TPU v7x, 32 devices: a whole 2x2x4 slice. The times are simulated.
32 devices in a mesh: grp: 8 (over z, x), inner: 4 (over y, core).
Axes of the slice: x: 2, y: 2, z: 4, core: 2. Of those that a mesh axis runs over, the one named last changes fastest.
Arguments:
- signal: bfloat16 [64, 1024, 4096], P('grp', None, 'inner'), may hold values from -6 to 6
- bins: int32 [8], replicated, may hold values from 1 to 512, as said below
- mic_positions: float32 [3, 4096], replicated, may hold values from -1 to 1
- grid_positions: float32 [3, 1024], replicated, may hold values from 1 to 3
Outputs:
- beam_map: float32 [8, 1024], replicated
Inputs may be any that keep to these rules, and one draw needn't show every extreme that they name: The 8 bins are distinct; bin 1 and bin 1024 / 2 are always among them.
All inputs are finite; a program needn't handle non-finite values.
Results may differ from a plain program's by a relative error of at most 0.02.
Values may be sent and summed in bfloat16 or wider, within the bound.
No kernel may reach another device: no remote copies, remote signals or barrier semaphores. Data moves between devices by JAX's collectives and lax.ppermute only.
A program may use at most 192 MiB of HBM per device.

v0:
```python
import math

import jax
import jax.numpy as jnp
from jax import lax
from jax.sharding import PartitionSpec as P

SAMPLES = 1024
F = 8


TWO_PI = 2.0 * math.pi
RATE_OVER_SOUND = 51200.0 / 343.0


def dft_table(bins):
    ticks = jnp.arange(SAMPLES, dtype=jnp.int32)
    turns = bins[:, None] * ticks[None, :] % SAMPLES
    angle = turns.astype(jnp.float32) * (TWO_PI / SAMPLES)
    window = 0.5 - 0.5 * jnp.cos(ticks.astype(jnp.float32) * (TWO_PI / SAMPLES))
    factor = math.sqrt(8.0 / (3.0 * SAMPLES))
    real_part = window[None, :] * jnp.cos(angle) * factor
    imag_part = -window[None, :] * jnp.sin(angle) * factor
    return jnp.concatenate([real_part, imag_part], 0).astype(jnp.bfloat16)


def distances(spots, grid):
    delta_x = grid[0][None, :] - spots[0][:, None]
    delta_y = grid[1][None, :] - spots[1][:, None]
    delta_z = grid[2][None, :] - spots[2][:, None]
    return jnp.sqrt(delta_x * delta_x + delta_y * delta_y + delta_z * delta_z) * RATE_OVER_SOUND


def steering(delay, frequency_bin):
    angle = delay * (frequency_bin.astype(jnp.float32) * (TWO_PI / SAMPLES))
    return jnp.concatenate([jnp.cos(angle), -jnp.sin(angle)], 0).astype(jnp.bfloat16)


def shards(signal, bins, mic_positions, grid_positions):
    table = dft_table(bins)
    local = jnp.einsum("kt,stm->skm", table, signal, preferred_element_type=jnp.float32).astype(
        jnp.bfloat16
    )
    snap_dev = local.shape[0]
    mic_cols = local.shape[2]
    local = local.reshape(snap_dev, 2, F, mic_cols)
    grp_size = lax.axis_size("grp")
    grp_index = lax.axis_index("grp")
    inner_index = lax.axis_index("inner")
    total_mics = mic_positions.shape[1]
    snaps = snap_dev * grp_size
    col_pos = lax.dynamic_slice_in_dim(mic_positions, inner_index * mic_cols, mic_cols, 1)
    col_delay = distances(col_pos, grid_positions)
    wide = lax.all_gather(local, "inner", axis=3, tiled=True)
    rows = lax.all_to_all(wide, "grp", split_axis=3, concat_axis=0, tiled=True)
    row_count = rows.shape[3]
    row_ids = grp_index * row_count + jnp.arange(row_count, dtype=jnp.int32)
    row_pos = lax.dynamic_slice_in_dim(mic_positions, grp_index * row_count, row_count, 1)
    col_ids = inner_index * mic_cols + jnp.arange(mic_cols, dtype=jnp.int32)
    row_delay = distances(row_pos, grid_positions)
    piece = lax.all_gather(local, "grp", axis=0, tiled=True)
    real_rows = rows[:, 0]
    imag_rows = rows[:, 1]
    real_cols = piece[:, 0]
    imag_cols = piece[:, 1]
    form = "sfm,sfn->fmn"
    real_sum = jnp.einsum(
        form, real_rows, real_cols, preferred_element_type=jnp.float32
    ) + jnp.einsum(form, imag_rows, imag_cols, preferred_element_type=jnp.float32)
    imag_sum = jnp.einsum(
        form, imag_rows, real_cols, preferred_element_type=jnp.float32
    ) - jnp.einsum(form, real_rows, imag_cols, preferred_element_type=jnp.float32)
    diagonal_mask = row_ids[:, None] == col_ids[None, :]
    partial_value = []
    for index in range(F):
        real_c = jnp.where(diagonal_mask, 0.0, real_sum[index] / snaps)
        imag_c = jnp.where(diagonal_mask, 0.0, imag_sum[index] / snaps)
        block = jnp.concatenate(
            [jnp.concatenate([real_c, -imag_c], 1), jnp.concatenate([imag_c, real_c], 1)], 0
        )
        col_steer = steering(col_delay, bins[index]).astype(jnp.float32)
        row_steer = steering(row_delay, bins[index]).astype(jnp.float32)
        image = jnp.dot(
            block, col_steer, precision=lax.Precision.HIGHEST, preferred_element_type=jnp.float32
        )
        partial_value.append(jnp.sum(row_steer * image, axis=0))
    partial_value = jnp.stack(partial_value, 0)
    total = lax.psum(partial_value, ("grp", "inner"))
    return total * (math.sqrt(snaps) / total_mics)


def solution(mesh):
    in_specs = (P("grp", None, "inner"), P(), P(), P())
    out_specs = P()
    return jax.shard_map(shards, mesh=mesh, in_specs=in_specs, out_specs=out_specs, check_vma=False)
```

profile of v0, /device:TPU:0, one launch (start us, length us, event | category | flops | bytes accessed | tf_op | source)
XLA Modules:
  0.0 594.0 jit_solution(5859230834884939735)
XLA Ops:
  6.5 0.0 all-gather.3.cloned.1.call-start
  6.6 0.9 multiply_convert_fusion.1
  7.5 0.0 copy-start.1
  7.5 0.0 copy-start.2
  7.5 8.8 %fusion.136 = bf16[8,2,8,1024]{3,2,1,0:T(8,128)(2,1)} fusion(bf16[8,1024,1024]{2,1,0:T(8,128)(2,1)} %param.4, bf16[8,1024]{1,0:T(8,128)(2,1)S(1)} %get-tuple-element.101, bf16[8,1024]{1,0:T(8,128)(2,1)S(1)} %get-tuple-element.100), kind=kOutput, calls=%fused_computation.181 | convolution fusion | flops 268632064 | bytes 17072128 | tf_op jit(solution)/shard_map/kt,stm->skm/dot_general | solution.py:41
  16.3 0.0 all-gather.3.cloned.1.call-update
  16.3 0.0 all-gather.5.cloned.1.call-start
  16.3 1.8 copy.12
  18.1 0.0 all-gather.5.cloned.1.call-update
  18.2 0.0 copy-done.1
  18.2 0.7 fusion.174
  23.9 0.9 constant_dynamic-slice_fusion
  24.8 0.9 constant_dynamic-slice_fusion.1
  25.7 0.0 copy-done.2
  25.8 10.1 %all-gather.3.cloned.1.call-done = bf16[8,2,8,4096]{3,2,1,0:T(8,128)(2,1)} async-done(((bf16[8,2,8,1024]{3,2,1,0:T(8,128)(2,1)}), bf16[8,2,8,4096]{3,2,1,0:T(8,128)(2,1)}) %all-gather.3.cloned.1.call-update) | async-done | bytes 1048592 | tf_op jit(solution)/shard_map/all_gather | solution.py:54
  35.9 32.9 %copy.10 = bf16[8,2,8,4096]{2,1,0,3:T(2,128)(2,1)} copy(bf16[8,2,8,4096]{3,2,1,0:T(8,128)(2,1)} %all-gather.3.cloned.1.call-done) | data formatting | bytes 2097152 | tf_op jit(solution)/shard_map/all_gather | solution.py:54
  68.7 20.5 %reshape.88 = bf16[8,2,32768]{2,1,0:T(2,128)(2,1)} reshape(bf16[4096,8,2,8]{3,2,1,0:T(2,128)(2,1)} %bitcast.127) | data formatting | bytes 2097152
  89.2 5.5 all-to-all-start
  94.7 64.9 %cosine_convert_fusion.8 = (bf16[512,1024]{1,0:T(8,128)(2,1)}, bf16[512,1024]{1,0:T(8,128)(2,1)}, bf16[512,1024]{1,0:T(8,128)(2,1)}, bf16[512,1024]{1,0:T(8,128)...) fusion(f32[]{:T(128)} %bitcast.49, ...), kind=kLoop, calls=%fused_computation.164 | loop fusion | flops 20971520 | bytes 16795680 | tf_op jit(solution)/shard_map/convert.2
  159.6 127.8 %cosine_convert_fusion = (bf16[1024,1024]{1,0:T(8,128)(2,1)}, bf16[1024,1024]{1,0:T(8,128)(2,1)}, bf16[1024,1024]{1,0:T(8,128)(2,1)}, bf16[1024,1024]{1,0:T(8,12...) fusion(f32[]{:T(128)} %bitcast.49, ...), kind=kLoop, calls=%fused_computation.108 | loop fusion | flops 41943040 | bytes 33579040 | tf_op jit(solution)/shard_map/convert
  287.4 0.0 all-to-all-done
  287.4 20.7 %reshape.89 = bf16[4096,8,2,8]{3,2,1,0:T(2,128)(2,1)} reshape(bf16[8,2,32768]{2,1,0:T(2,128)(2,1)S(1)} %all-to-all-done) | data formatting | bytes 2097152
  308.1 24.9 %copy.11 = bf16[8,2,8,8,512]{4,0,3,2,1:T(8,128)(2,1)S(1)} copy(bf16[8,2,8,8,512]{2,1,0,4,3:T(2,128)(2,1)} %bitcast.128) | data formatting | bytes 2097152 | tf_op jit(solution)/shard_map/all_to_all | solution.py:55
  333.0 0.0 all-gather.5.cloned.1.call-done
  333.0 0.0 copy-start
  333.0 9.5 %fusion.137 = f32[8,512,1024]{2,1,0:T(8,128)} fusion(bf16[64,2,8,1024]{3,0,2,1:T(8,128)(2,1)} %all-gather.5.cloned.1.call-done, bf16[64,2,8,512]{3,0,2,1:T(8,128)(2,1)S(1)} %bitcast.129), kind=kOutput, calls=%fused_computation.184 | convolution fusion | flops 536870912 | bytes 18350080 | tf_op jit(solution)/shard_map/sfm,sfn->fmn/dot_general | solution.py:70
  342.5 0.0 copy-done
  342.5 2.4 fusion.138
  344.9 14.2 %convolution_subtract_fusion = f32[8,512,1024]{2,1,0:T(8,128)} fusion(f32[8,512,1024]{2,1,0:T(8,128)} %fusion.137, bf16[64,2,8,1024]{3,0,2,1:T(8,128)(2,1)} %all-gather.5.cloned.1.call-done, bf16[64,2,8,512]{3,0,2,1:T(8,128)(2,1)S(1)} %bitcast.131), kind=kOutput, calls=%fused_computation.16 | convolution fusion | flops 541065216 | bytes 35127296 | tf_op jit(solution)/shard_map/sfm,sfn->fmn/dot_general | solution.py:72
  359.1 9.4 %convolution_add_fusion = f32[8,512,1024]{2,1,0:T(8,128)} fusion(f32[8,512,1024]{2,1,0:T(8,128)S(1)} %fusion.138, bf16[64,2,8,1024]{3,0,2,1:T(8,128)(2,1)} %all-gather.5.cloned.1.call-done, bf16[64,2,8,512]{3,0,2,1:T(8,128)(2,1)S(1)} %bitcast.132), kind=kOutput, calls=%fused_computation.17 | convolution fusion | flops 541065216 | bytes 35127296 | tf_op jit(solution)/shard_map/sfm,sfn->fmn/dot_general | solution.py:69
  368.4 24.9 %fusion.165 = (f32[512,1024]{1,0:T(8,128)S(1)}, f32[512,1024]{1,0:T(8,128)S(1)}, f32[512,1024]{1,0:T(8,128)}, f32[512,1024]{1,0:T(8,128)}, f32[512,1024]{1,0:T(8...) fusion(f32[8,512,1024]{2,1,0:T(8,128)} %convolution_subtract_fu, ...), kind=kLoop, calls=%fused_computation.226 | loop fusion | flops 21495808 | bytes 83892224 | tf_op jit(solution)/shard_map/neg | solution.py:79
  393.3 19.5 %multiply_reduce_fusion.1 = f32[1024]{0:T(1024)S(1)} fusion(bf16[512,1024]{1,0:T(8,128)(2,1)} %get-tuple-element.72, bf16[512,1024]{1,0:T(8,128)(2,1)} %get-tuple-element.73, bf16[1024,1024]{1,0:T(8,128)(2,1)} %get-tuple-element.56, bf16[1024,1024]{1,0:T(8,128)(2,1)} %get-tuple-element.57, f32[512,1024]{1,0:T(8,128)} %get-tuple-element.90, ...), kind=kOutput, calls=%fused_computation.109 | convolution fusion | flops 25790775296 | bytes 12587008 | tf_op jit(solution)/shard_map/dot_general | solution.py:83
  412.8 19.5 %multiply_reduce_fusion.2 = f32[1024]{0:T(1024)S(1)} fusion(bf16[512,1024]{1,0:T(8,128)(2,1)} %get-tuple-element.71, bf16[512,1024]{1,0:T(8,128)(2,1)} %get-tuple-element.74, bf16[1024,1024]{1,0:T(8,128)(2,1)} %get-tuple-element.55, bf16[1024,1024]{1,0:T(8,128)(2,1)} %get-tuple-element.58, f32[512,1024]{1,0:T(8,128)} %get-tuple-element.89, ...), kind=kOutput, calls=%fused_computation.112 | convolution fusion | flops 25790775296 | bytes 12587008 | tf_op jit(solution)/shard_map/dot_general | solution.py:83
  432.3 19.8 %multiply_reduce_fusion.3 = f32[1024]{0:T(1024)S(1)} fusion(bf16[512,1024]{1,0:T(8,128)(2,1)} %get-tuple-element.70, bf16[512,1024]{1,0:T(8,128)(2,1)} %get-tuple-element.75, bf16[1024,1024]{1,0:T(8,128)(2,1)} %get-tuple-element.54, bf16[1024,1024]{1,0:T(8,128)(2,1)} %get-tuple-element.59, f32[512,1024]{1,0:T(8,128)} %get-tuple-element.88, ...), kind=kOutput, calls=%fused_computation.115 | convolution fusion | flops 25790775296 | bytes 12587008 | tf_op jit(solution)/shard_map/dot_general | solution.py:83
  452.1 19.5 %multiply_reduce_fusion.4 = f32[1024]{0:T(1024)S(1)} fusion(bf16[512,1024]{1,0:T(8,128)(2,1)} %get-tuple-element.69, bf16[512,1024]{1,0:T(8,128)(2,1)} %get-tuple-element.76, bf16[1024,1024]{1,0:T(8,128)(2,1)} %get-tuple-element.53, bf16[1024,1024]{1,0:T(8,128)(2,1)} %get-tuple-element.60, f32[512,1024]{1,0:T(8,128)} %get-tuple-element.87, ...), kind=kOutput, calls=%fused_computation.118 | convolution fusion | flops 25790775296 | bytes 12587008 | tf_op jit(solution)/shard_map/dot_general | solution.py:83
  471.6 19.5 %multiply_reduce_fusion.5 = f32[1024]{0:T(1024)S(1)} fusion(bf16[512,1024]{1,0:T(8,128)(2,1)} %get-tuple-element.68, bf16[512,1024]{1,0:T(8,128)(2,1)} %get-tuple-element.77, bf16[1024,1024]{1,0:T(8,128)(2,1)} %get-tuple-element.52, bf16[1024,1024]{1,0:T(8,128)(2,1)} %get-tuple-element.61, f32[512,1024]{1,0:T(8,128)} %get-tuple-element.86, ...), kind=kOutput, calls=%fused_computation.121 | convolution fusion | flops 25790775296 | bytes 12587008 | tf_op jit(solution)/shard_map/dot_general | solution.py:83
  491.1 19.5 %multiply_reduce_fusion.6 = f32[1024]{0:T(1024)S(1)} fusion(bf16[512,1024]{1,0:T(8,128)(2,1)} %get-tuple-element.67, bf16[512,1024]{1,0:T(8,128)(2,1)} %get-tuple-element.78, bf16[1024,1024]{1,0:T(8,128)(2,1)} %get-tuple-element.51, bf16[1024,1024]{1,0:T(8,128)(2,1)} %get-tuple-element.62, f32[512,1024]{1,0:T(8,128)} %get-tuple-element.85, ...), kind=kOutput, calls=%fused_computation.124 | convolution fusion | flops 25790775296 | bytes 12587008 | tf_op jit(solution)/shard_map/dot_general | solution.py:83
  510.7 17.4 %multiply_reduce_fusion = f32[1024]{0:T(1024)S(1)} fusion(bf16[512,1024]{1,0:T(8,128)(2,1)} %get-tuple-element.80, bf16[512,1024]{1,0:T(8,128)(2,1)} %get-tuple-element.65, bf16[1024,1024]{1,0:T(8,128)(2,1)} %get-tuple-element.64, bf16[1024,1024]{1,0:T(8,128)(2,1)} %get-tuple-element.49, f32[512,1024]{1,0:T(8,128)} %get-tuple-element.91, ...), kind=kOutput, calls=%fused_computation.106 | convolution fusion | flops 25790775296 | bytes 12587008 | tf_op jit(solution)/shard_map/dot_general | solution.py:83
  528.1 17.8 %multiply_reduce_fusion.7 = f32[1024]{0:T(1024)S(1)} fusion(bf16[512,1024]{1,0:T(8,128)(2,1)} %get-tuple-element.66, bf16[512,1024]{1,0:T(8,128)(2,1)} %get-tuple-element.79, bf16[1024,1024]{1,0:T(8,128)(2,1)} %get-tuple-element.50, bf16[1024,1024]{1,0:T(8,128)(2,1)} %get-tuple-element.63, f32[512,1024]{1,0:T(8,128)} %get-tuple-element.84, ...), kind=kOutput, calls=%fused_computation.127 | convolution fusion | flops 25790775296 | bytes 12587008 | tf_op jit(solution)/shard_map/dot_general | solution.py:83
  545.9 0.1 stack.35
  546.0 40.0 %psum.7 = f32[8,1024]{1,0:T(8,128)S(1)} all-reduce(f32[8,1024]{1,0:T(8,128)S(1)} %stack.35), channel_id=1, replica_groups=mesh['grp'=8,'inner'=4] {'grp','inner'}, use_global_device_ids=true, to_apply=%region_8.9 | all-reduce | flops 8192 | bytes 65536 | tf_op jit(solution)/shard_map/psum | solution.py:88
  586.0 0.6 broadcast_multiply_fusion
  (4 shorter events, 0.1 us)
Async XLA Ops:
  6.5 29.3 %all-gather.3.cloned.1.call-start = ((), (), s32[]{:S(2)}) async-start(), calls=%async_computation.1 | async-start | bytes 1310720 | tf_op jit(solution)/shard_map/all_gather | solution.py:54
  7.5 10.7 %copy-start.1 = (s32[8]{0:T(128)S(1)}, s32[8]{0:T(128)}, u32[]{:S(2)}) copy-start(s32[8]{0:T(128)} %param.5) | copy-start | bytes 100
  7.5 18.3 %copy-start.2 = (f32[3,1024]{1,0:T(4,128)S(1)}, f32[3,1024]{1,0:T(4,128)}, u32[]{:S(2)}) copy-start(f32[3,1024]{1,0:T(4,128)} %param.7) | copy-start | bytes 36868
  16.3 316.7 %all-gather.5.cloned.1.call-start = ((), (), s32[]{:S(2)}) async-start(), calls=%async_computation.2 | async-start | bytes 2359296 | tf_op jit(solution)/shard_map/all_gather | solution.py:61
  89.2 198.2 %all-to-all-start = ((bf16[8,2,32768]{2,1,0:T(2,128)(2,1)}), bf16[8,2,32768]{2,1,0:T(2,128)(2,1)S(1)}, u32[]{:S(2)}, u32[]{:S(2)}) async-start(bf16[8,2,32768]{2,1,0:T(2,128)(2,1)} %reshape.88), calls=%async_computation | async-start | bytes 2097152 | tf_op jit(solution)/shard_map/all_to_all | solution.py:55
  333.0 9.5 %copy-start = (bf16[64,2,8,1024]{3,0,2,1:T(8,128)(2,1)S(1)}, bf16[64,2,8,1024]{3,0,2,1:T(8,128)(2,1)}, u32[]{:S(2)}) copy-start(bf16[64,2,8,1024]{3,0,2,1:T(8,128)(2,1)} %all-gather.5.cloned.1.call-done) | copy-start | bytes 6291460
Sparse Core Ops, SparseCore 0:
  16.4 19.4 all-gather.2
  38.0 49.2 all-gather.4
where the time goes:
time: 605 us; the launch traced here: 594 us
  other arithmetic  219 us (36%)
  matrix products  197 us (33%)
  local copies, waits for them, and re-layouts  103 us (17%)
  blocking collectives  40 us (7%)
  between operations  19.1 us (3%)
  waiting for transfers between devices  10.1 us (2%)
    another operation x3, other arithmetic  194 us
    dot_general x8, matrix products, shards(): jnp.dot(block, col_steer, precision=lax.Precision.HIGHEST, preferred_elem...  153 us
    unnamed x8, local copies, waits for them, and re-layouts  41.2 us
    psum x1, blocking collectives, shards(): total = lax.psum(partial_value, ('grp', 'inner'))  40 us
    all_gather x1, local copies, waits for them, and re-layouts, shards(): wide = lax.all_gather(local, 'inner', axis=3, tiled=True)  32.9 us
    all_to_all x1, local copies, waits for them, and re-layouts, shards(): rows = lax.all_to_all(wide, 'grp', split_axis=3, concat_axis=0, tiled=True)  24.9 us
    neg x1, other arithmetic, shards(): -imag_c  24.9 us
    dot_general x1, matrix products, shards(): jnp.einsum(form, real_rows, imag_cols, preferred_element_type=jnp.float32)  14.2 us
  transfers between devices with their start and end apart: 3, of which 1 were waited for; matrix products, arithmetic and copies ran while one was open for 50% of the time, Pallas kernels for 0%

commit v1 on v0

v1 whole, which is shorter than its diff:
```python
import functools
import math

import jax
import jax.numpy as jnp
from jax import lax
from jax.experimental import pallas as pl
from jax.experimental.pallas import tpu as pltpu
from jax.sharding import Mesh, PartitionSpec as P

F = 8
TWO_PI = 2.0 * math.pi
RATE_OVER_SOUND = 51200.0 / 343.0
F32 = jnp.float32
BF16 = jnp.bfloat16
ROUNDER = 12582912.0
LANES = 128

SIN_HALF = (4.4428679027342115, -7.307443409650812, 3.5947879684072226, -0.7843737403612829)
COS_HALF = (1.414204080247352, -6.9776420363098905, 5.715238127798347, -1.7283478206531864)
SIN_FINE = (4.442882937668975, -7.308249445082402, 3.6064748105185624, -0.8474638068718637, 0.11600967661123661, -0.009900200019037797)
COS_FINE = (1.4142135623720369, -6.978864199223495, 5.739885708320473, -1.8883460768140574, 0.33280043358005373, -0.036453250292718266, 0.0026021832760962107)


def polynomial(coefs, u):
    value = coefs[-1] * u + coefs[-2]
    for c in coefs[-3::-1]:
        value = value * u + c
    return value


def cos_sin(turns, sin_half=SIN_HALF, cos_half=COS_HALF):
    r = turns - ((turns + ROUNDER) - ROUNDER)
    u = r * r
    s = polynomial(sin_half, u) * r
    c = polynomial(cos_half, u)
    return 1.0 - s * s, s * c


def dft_table(bins_ref, samples):
    shape = (F, samples)
    row = lax.broadcasted_iota(jnp.int32, shape, 0)
    ticks = lax.broadcasted_iota(jnp.int32, shape, 1)
    bins = jnp.zeros(shape, jnp.int32)
    for f in range(F):
        bins = jnp.where(row == f, bins_ref[f], bins)
    turns = ((bins * ticks) & (samples - 1)).astype(F32) * (1.0 / samples)
    half = ticks.astype(F32) * (1.0 / samples)
    half = half - ((half + ROUNDER) - ROUNDER)
    half_sin = polynomial(SIN_FINE, half * half) * half
    window = 0.5 * half_sin * half_sin * math.sqrt(8.0 / (3.0 * samples))
    cos, sin = cos_sin(turns, SIN_FINE, COS_FINE)
    return jnp.concatenate([window * cos, -window * sin], 0).astype(BF16)


def spread_grid(grid_ref, spread, first):
    for k in range(3):
        for block in range(spread.shape[1] // LANES):
            start = pl.multiple_of(first + block * LANES, LANES)
            line = grid_ref[k : k + 1, pl.ds(start, LANES)]
            spread[k, block * LANES : (block + 1) * LANES, :] = jnp.broadcast_to(line, (LANES, LANES)).T


def steer_rows(row, scale, mic_ref, mic_start, spread, out_row, cos_ref, sin_ref):
    rows = pl.ds(row, 16)
    gx, gy, gz = spread[0, rows, :], spread[1, rows, :], spread[2, rows, :]
    out_rows = pl.ds(out_row, 16)
    at = 0
    for start, width in mic_start:
        for lane in range(0, width, LANES):
            lanes = pl.ds(pl.multiple_of(start + lane, LANES), LANES)
            dx = gx - mic_ref[0:1, lanes]
            dy = gy - mic_ref[1:2, lanes]
            dz = gz - mic_ref[2:3, lanes]
            square = dx * dx + dy * dy + dz * dz
            turns = square * lax.rsqrt(jnp.maximum(square, 1e-30)) * scale
            cos, sin = cos_sin(turns)
            cos_ref[out_rows, at : at + LANES] = cos.astype(BF16)
            sin_ref[out_rows, at : at + LANES] = sin.astype(BF16)
            at += LANES


def mic_order(pairs, width, core):
    return [((2 * pair + lax.rem(core + h, 2)) * width, width) for h in range(2) for pair in range(pairs)]


def turns_per_metre(bins_ref, index, samples):
    return bins_ref[index].astype(F32) * (RATE_OVER_SOUND / samples)


def dft_kernel(pairs, place_ref, bins_ref, mic_ref, grid_ref, signal_ref, out_ref, cos_ref, sin_ref, held, total, spread, sem):
    snaps, samples, mics = held.shape

    def copy(s):
        return pltpu.make_async_copy(signal_ref.at[s], held.at[s], sem.at[s])

    for s in range(snaps):
        copy(s).start()
    index, core = place_ref[0], place_ref[1]
    table = dft_table(bins_ref, samples)
    points = cos_ref.shape[0]
    spread_grid(grid_ref, spread, core * (grid_ref.shape[1] // 2))
    scale = turns_per_metre(bins_ref, index, samples)
    order = mic_order(pairs, mics, core)
    each = points // snaps

    def step(s, carry):
        copy(s).wait()
        total[:, pl.ds(s, 1), :] = jnp.dot(table, held[s], preferred_element_type=F32)[:, None, :]
        for part in range(0, each, 16):
            row = pl.multiple_of(s * each + part, 16)
            steer_rows(row, scale, mic_ref, order, spread, row, cos_ref, sin_ref)
        return carry

    lax.fori_loop(0, snaps, step, 0)
    for f in range(F):
        out_ref[f] = jnp.concatenate([total[f], total[F + f]], 0).astype(BF16)


def steer_kernel(pairs, first, samples, mics, place_ref, bins_ref, mic_ref, grid_ref, cos_ref, sin_ref, spread):
    index, core = place_ref[0], place_ref[1]
    spread_grid(grid_ref, spread, core * (grid_ref.shape[1] // 2) + first)
    scale = turns_per_metre(bins_ref, index, samples)
    order = mic_order(pairs, mics, core)

    def step(i, carry):
        row = pl.multiple_of(i * 16, 16)
        steer_rows(row, scale, mic_ref, order, spread, row, cos_ref, sin_ref)
        return carry

    lax.fori_loop(0, cos_ref.shape[0] // 16, step, 0)


def project_kernel(nears, pairs, own_ref, other_ref, cos_a_ref, sin_a_ref, cos_b_ref, sin_b_ref, out_ref, real_lhs, swap_lhs, power):
    blocks, rows, mics = own_ref.shape
    half = rows // 2
    wide = real_lhs.shape[0]
    real_lhs[...] = jnp.zeros_like(real_lhs)
    swap_lhs[...] = jnp.zeros_like(swap_lhs)
    at = 0
    for ref in (own_ref, other_ref):
        for pair in range(pairs):
            line = jnp.zeros((1, mics), F32)
            for near in range(nears):
                block = ref[near * pairs + pair].astype(F32)
                real_lhs[near * rows : (near + 1) * rows, at : at + mics] = block.astype(BF16)
                swapped = jnp.concatenate([-block[half:], block[:half]], 0)
                swap_lhs[near * rows : (near + 1) * rows, at : at + mics] = swapped.astype(BF16)
                line = line + jnp.sum(block * block, axis=0, keepdims=True)
            power[:, at : at + mics] = jnp.broadcast_to(line, (8, mics))
            at += mics
    point = 0
    chunk = 128
    form = (((1,), (1,)), ((), ()))
    for cos_ref, sin_ref in ((cos_a_ref, sin_a_ref), (cos_b_ref, sin_b_ref)):
        for start in range(0, cos_ref.shape[0], chunk):
            cos = cos_ref[start : start + chunk, :]
            sin = sin_ref[start : start + chunk, :]
            y = lax.dot_general(cos, real_lhs[...], form, preferred_element_type=F32)
            y = y + lax.dot_general(sin, swap_lhs[...], form, preferred_element_type=F32)
            lane_sums = []
            for row in range(0, chunk, 16):
                acc = jnp.zeros((16, LANES), F32)
                for lane in range(0, at, LANES):
                    c = cos_ref[start + row : start + row + 16, lane : lane + LANES].astype(F32)
                    d = sin_ref[start + row : start + row + 16, lane : lane + LANES].astype(F32)
                    acc = acc + (c * c + d * d) * power[0:1, lane : lane + LANES]
                lane_sums.append(acc)
            diagonal = jnp.concatenate(lane_sums, 0)
            value = y * y
            part = value[:, :LANES]
            for lane in range(LANES, wide, LANES):
                part = part + value[:, lane : lane + LANES]
            line = jnp.sum((part - diagonal).T, axis=0, keepdims=True)
            out_ref[:, point // LANES : point // LANES + 1, :] = jnp.broadcast_to(line[None], (out_ref.shape[0], 1, LANES))
            point += chunk


def shards(nears, pairs, devices, signal, bins, mic_positions, grid_positions):
    snaps, samples, mics = signal.shape
    total_mics = mic_positions.shape[1]
    points = grid_positions.shape[1]
    half_points = points // 2
    shadow = half_points // 2
    rest = half_points - shadow
    core = lax.axis_index("core")
    place = jnp.stack([lax.axis_index("near") * pairs + lax.axis_index("pair"), core]).astype(jnp.int32)
    vmem = pl.BlockSpec(memory_space=pltpu.VMEM)
    smem = pl.BlockSpec(memory_space=pltpu.SMEM)
    params = pltpu.CompilerParams(vmem_limit_bytes=40 * 2**20)
    steer_cost = pl.CostEstimate(flops=40 * rest * total_mics, bytes_accessed=4 * rest * total_mics, transcendentals=rest * total_mics)
    steer_shape = [jax.ShapeDtypeStruct((shadow, total_mics), BF16)] * 2
    local, cos_a, sin_a = pl.pallas_call(
        functools.partial(dft_kernel, pairs),
        in_specs=[smem, smem, vmem, vmem, pl.BlockSpec(memory_space=pl.ANY)],
        out_specs=[vmem] * 3,
        out_shape=[jax.ShapeDtypeStruct((F, 2 * snaps, mics), BF16)] + steer_shape,
        scratch_shapes=[
            pltpu.VMEM((snaps, samples, mics), BF16),
            pltpu.VMEM((2 * F, snaps, mics), F32),
            pltpu.VMEM((3, shadow, LANES), F32),
            pltpu.SemaphoreType.DMA((snaps,)),
        ],
        compiler_params=params,
        name="dft_and_steering",
    )(place, bins, mic_positions, grid_positions, signal)
    own = lax.all_to_all(local, ("near", "pair"), 0, 0, tiled=True)
    cos_b, sin_b = pl.pallas_call(
        functools.partial(steer_kernel, pairs, shadow, samples, mics),
        in_specs=[smem, smem, vmem, vmem],
        out_specs=[vmem] * 2,
        out_shape=[jax.ShapeDtypeStruct((rest, total_mics), BF16)] * 2,
        scratch_shapes=[pltpu.VMEM((3, rest, LANES), F32)],
        compiler_params=pltpu.CompilerParams(vmem_limit_bytes=16 * 2**20),
        cost_estimate=steer_cost,
        name="steering",
    )(place, bins, mic_positions, grid_positions)
    other = lax.ppermute(own, "core", [(0, 1), (1, 0)])
    rows = nears * 2 * snaps
    wide = -(-rows // LANES) * LANES
    mine = pl.pallas_call(
        functools.partial(project_kernel, nears, pairs),
        in_specs=[vmem] * 6,
        out_specs=vmem,
        out_shape=jax.ShapeDtypeStruct((devices, half_points // LANES, LANES), F32),
        scratch_shapes=[
            pltpu.VMEM((wide, total_mics), BF16),
            pltpu.VMEM((wide, total_mics), BF16),
            pltpu.VMEM((8, total_mics), F32),
        ],
        compiler_params=pltpu.CompilerParams(vmem_limit_bytes=24 * 2**20),
        name="projection",
    )(own, other, cos_a, sin_a, cos_b, sin_b)
    axes = ("wide", "near", "pair", "core")
    everyone = lax.all_to_all(mine, axes, 0, 0, tiled=True)
    summed = jnp.sum(everyone.reshape(-1, F, points), axis=0)
    all_snaps = snaps * lax.axis_size("wide") * nears
    return summed * (1.0 / (math.sqrt(all_snaps) * total_mics))


def solution(mesh):
    groups, inner = mesh.shape["grp"], mesh.shape["inner"]
    pairs = inner // 2
    nears = F // pairs
    fine = Mesh(mesh.devices.reshape(groups // nears, nears, pairs, 2), ("wide", "near", "pair", "core"))
    in_specs = (P(("wide", "near"), None, ("pair", "core")), P(), P(), P())
    step = functools.partial(shards, nears, pairs, groups * inner)
    return jax.shard_map(step, mesh=fine, in_specs=in_specs, out_specs=P(), check_vma=False)
```

time: 605 us -> 46.2 us (0.08); the launches traced: 594 us -> 45.9 us
  other arithmetic: 219 us -> 0.7 us
  matrix products: 197 us -> 0 us
  local copies, waits for them, and re-layouts: 103 us -> 2.24 us
  Pallas kernels: 0 us -> 19.6 us
  between operations: 19.1 us -> 0.05 us
  blocking collectives: 40 us -> 23.2 us
  waiting for transfers between devices: 10.1 us -> 0.01 us
    dot_general x13 -> x0, matrix products: 197 us -> none  [the longest x8 153 us: shards(): jnp.dot(block, col_steer, precision=lax.Precision.HIGHEST, preferred_elem...]
    another operation x3 -> x1, other arithmetic: 194 us -> 0.07 us  [shards(): jnp.stack([lax.axis_index('near') * pairs + lax.axis_index('pair'), core])]
    psum x1 -> x0, blocking collectives: 40 us -> none  [shards(): total = lax.psum(partial_value, ('grp', 'inner'))]
    unnamed x8 -> x6, local copies, waits for them, and re-layouts: 41.2 us -> 2.21 us
    all_gather x1 -> x0, local copies, waits for them, and re-layouts: 32.9 us -> none  [shards(): wide = lax.all_gather(local, 'inner', axis=3, tiled=True)]
    all_to_all x1 -> x0, local copies, waits for them, and re-layouts: 24.9 us -> none  [shards(): rows = lax.all_to_all(wide, 'grp', split_axis=3, concat_axis=0, tiled=True)]
    neg x1 -> x0, other arithmetic: 24.9 us -> none  [shards(): -imag_c]
    all_to_all x0 -> x2, blocking collectives: none -> 23.2 us  [the longest x1 12.6 us: shards(): own = lax.all_to_all(local, ('near', 'pair'), 0, 0, tiled=True)]
  transfers between devices with their start and end apart: 3 -> 1, of which waited for: 1 -> 0; matrix products, arithmetic and copies ran while one was open for 50% -> 0% of each run, Pallas kernels for 0% -> 12%
where the time goes in v1:
time: 46.2 us; the launch traced here: 45.9 us
  blocking collectives  23.2 us (50%)
  Pallas kernels  19.6 us (42%)
  local copies, waits for them, and re-layouts  2.24 us (5%)
  other arithmetic  0.7 us (2%)
    all_to_all x1, blocking collectives, shards(): own = lax.all_to_all(local, ('near', 'pair'), 0, 0, tiled=True)  12.6 us
    all_to_all x1, blocking collectives, shards(): everyone = lax.all_to_all(mine, axes, 0, 0, tiled=True)  10.6 us
    pallas_call x1, Pallas kernels, shards(): pl.pallas_call(functools.partial(dft_kernel, pairs), in_specs=[smem, smem...  10 us
    pallas_call x1, Pallas kernels, shards(): pl.pallas_call(functools.partial(steer_kernel, pairs, shadow, samples, mi...  5.48 us
    pallas_call x1, Pallas kernels, shards(): pl.pallas_call(functools.partial(project_kernel, nears, pairs), in_specs=...  4.13 us
    unnamed x6, local copies, waits for them, and re-layouts  2.21 us
  transfers between devices with their start and end apart: 1, of which 0 were waited for; matrix products, arithmetic and copies ran while one was open for 0% of the time, Pallas kernels for 12%

profile of v1, /device:TPU:0, one launch (start us, length us, event | category | flops | bytes accessed | tf_op | source)
XLA Modules:
  0.0 45.9 jit_solution(10312547336347303213)
XLA Ops:
  0.0 0.1 pad_add_fusion.place_ref
  0.1 0.0 copy-start
  0.1 0.8 %copy-done = f32[3,4096]{1,0:T(4,128)S(1)} copy-done((f32[3,4096]{1,0:T(4,128)S(1)}, f32[3,4096]{1,0:T(4,128)}, u32[]{:S(2)}) %copy-start) | copy-done | bytes 49176
  0.9 0.0 copy-start.1
  0.9 0.7 %copy-done.1 = f32[3,1024]{1,0:T(4,128)S(1)} copy-done((f32[3,1024]{1,0:T(4,128)S(1)}, f32[3,1024]{1,0:T(4,128)}, u32[]{:S(2)}) %copy-start.1) | copy-done | bytes 12312
  1.6 0.0 copy-start.2
  1.6 0.7 %copy-done.2 = s32[8]{0:T(128)S(1)} copy-done((s32[8]{0:T(128)S(1)}, s32[8]{0:T(128)}, u32[]{:S(2)}) %copy-start.2) | copy-done | bytes 56
  2.3 10.0 %dft_and_steering.1 = (bf16[8,16,1024]{2,1,0:T(8,128)(2,1)S(1)}, bf16[256,4096]{1,0:T(8,128)(2,1)S(1)}, bf16[256,4096]{1,0:T(8,128)(2,1)S(1)}) custom-call(s32[2]{0:T(128)S(1)} %pad_add_fusion.place_ref, s32[8]{0:T(128)S(1)} %copy-done.2, f32[3,4096]{1,0:T(4,128)S(1)} %copy-done, f32[3,1024]{1,0:T(4,128)S(1)} %copy-done.1, bf16[8,1024,1024]{2,1,0:T(8,128)(2,1)} %signal_ref.1), custom_call_target="tpu_custom_call" | custom-call | tf_op jit(solution)/shard_map/dft_and_steering/pallas_call | solution.py:193
  12.3 12.6 %all_to_all.10.own_ref = bf16[8,16,1024]{2,1,0:T(8,128)(2,1)S(1)} all-to-all(bf16[8,16,1024]{2,1,0:T(8,128)(2,1)S(1)} %get-tuple-element.10), channel_id=1, replica_groups=mesh['wide'=2,'near'=4,'pair'=2,'core'=2] {'near','pair'}, dimensions={0} | all-to-all | bytes 524288 | tf_op jit(solution)/shard_map/all_to_all | solution.py:207
  24.9 0.0 collective-permute-start
  24.9 5.5 %steering.1 = (bf16[256,4096]{1,0:T(8,128)(2,1)S(1)}, bf16[256,4096]{1,0:T(8,128)(2,1)S(1)}) custom-call(s32[2]{0:T(128)S(1)} %pad_add_fusion.place_ref, s32[8]{0:T(128)S(1)} %copy-done.2, f32[3,4096]{1,0:T(4,128)S(1)} %copy-done, f32[3,1024]{1,0:T(4,128)S(1)} %copy-done.1), custom_call_target="tpu_custom_call" | custom-call | flops 41943040 | bytes 4194304 | tf_op jit(solution)/shard_map/steering/pallas_call | solution.py:208
  30.4 0.0 collective-permute-done.other_ref
  30.4 4.1 %projection.1 = f32[32,4,128]{2,1,0:T(4,128)S(1)} custom-call(bf16[8,16,1024]{2,1,0:T(8,128)(2,1)S(1)} %all_to_all.10.own_ref, bf16[8,16,1024]{2,1,0:T(8,128)(2,1)S(1)} %collective-permute-done.other_ref, bf16[256,4096]{1,0:T(8,128)(2,1)S(1)} %get-tuple-element.11.cos_a_ref, bf16[256,4096]{1,0:T(8,128)(2,1)S(1)} %get-tuple-element.12.sin_a_ref, ...), custom_call_target="tpu_custom_call" | custom-call | tf_op jit(solution)/shard_map/projection/pallas_call | solution.py:221
  34.6 10.6 %all_to_all.11 = f32[32,4,128]{2,1,0:T(4,128)S(1)} all-to-all(f32[32,4,128]{2,1,0:T(4,128)S(1)} %projection.1), channel_id=1, replica_groups=mesh['wide'=2,'near'=4,'pair'=2,'core'=2] {'wide','near','pair','core'}, dimensions={0} | all-to-all | bytes 131072 | tf_op jit(solution)/shard_map/all_to_all | solution.py:235
  45.2 0.6 %broadcast_multiply_fusion = f32[8,1024]{1,0:T(8,128)} fusion(f32[8,1024]{1,0:T(8,128)S(1)} %reduce_sum.9), kind=kLoop, calls=%fused_computation | loop fusion | flops 8192 | bytes 65536 | tf_op jit(solution)/shard_map/mul | solution.py:238
  (2 shorter events, 0.0 us)
Async XLA Ops:
  0.1 0.8 %copy-start = (f32[3,4096]{1,0:T(4,128)S(1)}, f32[3,4096]{1,0:T(4,128)}, u32[]{:S(2)}) copy-start(f32[3,4096]{1,0:T(4,128)} %mic_ref.3) | copy-start | bytes 147460
  0.9 0.7 %copy-start.1 = (f32[3,1024]{1,0:T(4,128)S(1)}, f32[3,1024]{1,0:T(4,128)}, u32[]{:S(2)}) copy-start(f32[3,1024]{1,0:T(4,128)} %grid_ref.3) | copy-start | bytes 36868
  1.6 0.7 %copy-start.2 = (s32[8]{0:T(128)S(1)}, s32[8]{0:T(128)}, u32[]{:S(2)}) copy-start(s32[8]{0:T(128)} %bins_ref.3) | copy-start | bytes 100
  24.9 5.5 %collective-permute-start = (bf16[8,16,1024]{2,1,0:T(8,128)(2,1)S(1)}, bf16[8,16,1024]{2,1,0:T(8,128)(2,1)S(1)}, u32[]{:S(2)}, u32[]{:S(2)}) collective-permute-start(bf16[8,16,1024]{2,1,0:T(8,128)(2,1)S(1)} %all_to_all.10.own_ref), channel_id=1, source_target_pairs={{0,1},{1,0},{2,3},{3,2},{4,5},{5,4},{6,7},{7,6},{8,9},{9,8},{10,11... | collective-permute-start | bytes 786440 | tf_op jit(solution)/shard_map/ppermute | solution.py:218

commit v2 on v1

v2 whole, which is shorter than its diff:
```python
import functools
import math

import jax
import jax.numpy as jnp
from jax import lax
from jax.experimental import pallas as pl
from jax.experimental.pallas import tpu as pltpu
from jax.sharding import Mesh, PartitionSpec as P

F = 8
TWO_PI = 2.0 * math.pi
RATE_OVER_SOUND = 51200.0 / 343.0
F32 = jnp.float32
BF16 = jnp.bfloat16
ROUNDER = 12582912.0
LANES = 128
DEPTH = 64
STEP = 512
COLUMNS = 256

SIN_HALF = (4.4428679027342115, -7.307443409650812, 3.5947879684072226, -0.7843737403612829)
COS_HALF = (1.414204080247352, -6.9776420363098905, 5.715238127798347, -1.7283478206531864)
SIN_FINE = (4.442882937668975, -7.308249445082402, 3.6064748105185624, -0.8474638068718637, 0.11600967661123661, -0.009900200019037797)
COS_FINE = (1.4142135623720369, -6.978864199223495, 5.739885708320473, -1.8883460768140574, 0.33280043358005373, -0.036453250292718266, 0.0026021832760962107)


def polynomial(coefs, u):
    value = coefs[-1] * u + coefs[-2]
    for c in coefs[-3::-1]:
        value = value * u + c
    return value


def cos_sin(turns, sin_half=SIN_HALF, cos_half=COS_HALF):
    r = turns - ((turns + ROUNDER) - ROUNDER)
    u = r * r
    s = polynomial(sin_half, u) * r
    c = polynomial(cos_half, u)
    return 1.0 - s * s, s * c


def dft_table(bins_ref, samples):
    shape = (F, samples)
    row = lax.broadcasted_iota(jnp.int32, shape, 0)
    ticks = lax.broadcasted_iota(jnp.int32, shape, 1)
    bins = jnp.zeros(shape, jnp.int32)
    for f in range(F):
        bins = jnp.where(row == f, bins_ref[f], bins)
    turns = ((bins * ticks) & (samples - 1)).astype(F32) * (1.0 / samples)
    half = ticks.astype(F32) * (1.0 / samples)
    half = half - ((half + ROUNDER) - ROUNDER)
    half_sin = polynomial(SIN_FINE, half * half) * half
    window = 0.5 * half_sin * half_sin * math.sqrt(8.0 / (3.0 * samples))
    cos, sin = cos_sin(turns, SIN_FINE, COS_FINE)
    return jnp.concatenate([window * cos, -window * sin], 0).astype(BF16)


def split(value):
    high = value.astype(BF16).astype(F32)
    rest = value - high
    middle = rest.astype(BF16).astype(F32)
    return high, middle, rest - middle


def pairs_of(groups):
    return [jnp.concatenate([groups[i], groups[i + 1]], 0) for i in range(0, len(groups), 2)]


def distance_factors(scale, mic_ref, order, grid_ref, grid_start, rows8, left_ref, right_ref):
    at = 0
    for start, width in order:
        near = (1.0 - mic_ref[:, pl.ds(pl.multiple_of(start, LANES), width)]) * scale
        rows8[0:3, at : at + width] = near + near
        rows8[3:4, at : at + width] = jnp.sum(near * near, axis=0, keepdims=True)
        at += width
    rows8[4:5, :] = jnp.ones((1, at), F32)
    rows8[5:8, :] = jnp.zeros((3, at), F32)
    high, middle, low = split(rows8[...])
    for i, rows in enumerate(pairs_of([high, middle, low, high, middle, low, high, middle])):
        right_ref[16 * i : 16 * i + 16, :] = rows.astype(BF16)
    points = left_ref.shape[0]
    far = (grid_ref[:, pl.ds(pl.multiple_of(grid_start, LANES), points)] - 1.0) * scale
    rows8[0:3, :points] = far
    rows8[3:4, :points] = jnp.ones((1, points), F32)
    rows8[4:5, :points] = jnp.sum(far * far, axis=0, keepdims=True) + 1e-30
    high, middle, low = split(rows8[:, :points])
    groups = [high, high, high, middle, middle, middle, low, low]
    zeros = jnp.zeros((LANES - DEPTH, points), F32)
    left_ref[...] = jnp.concatenate(groups + [zeros], 0).T.astype(BF16)


def steer_rows(row, out_row, count, lanes, left_ref, right_ref, cos_ref, sin_ref):
    left = left_ref[pl.ds(row, count), 0:DEPTH]
    out_rows = pl.ds(out_row, count)
    step = lanes.step
    for at in lanes:
        square = jnp.dot(left, right_ref[0:DEPTH, at : at + step], preferred_element_type=F32)
        cos, sin = cos_sin(square * lax.rsqrt(square))
        cos_ref[out_rows, at : at + step] = cos.astype(BF16)
        sin_ref[out_rows, at : at + step] = sin.astype(BF16)


def mic_order(pairs, width, core):
    return [((2 * pair + lax.rem(core + h, 2)) * width, width) for h in range(2) for pair in range(pairs)]


def dft_kernel(
    pairs, place_ref, bins_hbm, mic_hbm, grid_hbm, signal_ref,
    out_ref, cos_ref, sin_ref, left_ref, right_ref,
    held, total, bins_ref, mic_ref, grid_ref, rows8, small_sem, sem,
):
    snaps, samples, mics = held.shape
    small = [
        pltpu.make_async_copy(source, target, small_sem.at[i])
        for i, (source, target) in enumerate([(bins_hbm, bins_ref), (mic_hbm, mic_ref), (grid_hbm, grid_ref)])
    ]

    def copy(s):
        return pltpu.make_async_copy(signal_ref.at[s], held.at[s], sem.at[s])

    for c in small:
        c.start()
    for s in range(snaps):
        copy(s).start(priority=1)
    for c in small:
        c.wait()
    index, core = place_ref[0], place_ref[1]
    scale = bins_ref[index].astype(F32) * (RATE_OVER_SOUND / samples)
    order = mic_order(pairs, mics, core)
    distance_factors(scale, mic_ref, order, grid_ref, core * (grid_ref.shape[1] // 2), rows8, left_ref, right_ref)
    table = dft_table(bins_ref, samples)
    each = cos_ref.shape[0] // snaps
    parts = max(mics // COLUMNS, 1)
    columns = mics // parts
    width = right_ref.shape[1] // parts

    def steer(s, part):
        row = pl.multiple_of(s * each, 16)
        lanes = range(part * width, (part + 1) * width, min(STEP, width))
        steer_rows(row, row, each, lanes, left_ref, right_ref, cos_ref, sin_ref)

    def transform(s, part):
        across = slice(part * columns, (part + 1) * columns)
        total[:, pl.ds(s, 1), across] = jnp.dot(table, held[s, :, across], preferred_element_type=F32)[:, None, :]

    def step(s, carry):
        copy(s).wait()
        for part in range(parts):
            transform(s, part)
            steer(s + 1, part)
        return carry

    for part in range(parts):
        steer(0, part)
    lax.fori_loop(0, snaps - 1, step, 0)
    copy(snaps - 1).wait()
    for part in range(parts):
        transform(snaps - 1, part)
    for f in range(F):
        out_ref[f] = jnp.concatenate([total[f], total[F + f]], 0).astype(BF16)


def project(nears, pairs, side, x_ref, cos_ref, sin_ref, real_lhs, swap_lhs, power, use):
    blocks, rows, mics = x_ref.shape
    half = rows // 2
    used = nears * rows
    if used < real_lhs.shape[0]:
        real_lhs[used:, :] = jnp.zeros((real_lhs.shape[0] - used, real_lhs.shape[1]), BF16)
        swap_lhs[used:, :] = jnp.zeros((real_lhs.shape[0] - used, real_lhs.shape[1]), BF16)
    for pair in range(pairs):
        lanes = slice(pair * mics, (pair + 1) * mics)
        squares = jnp.zeros((half, mics), F32)
        for near in range(nears):
            block = x_ref[near * pairs + pair]
            real_lhs[near * rows : (near + 1) * rows, lanes] = block
            block = block.astype(F32)
            top, low = block[:half], block[half:]
            swap_lhs[near * rows : (near + 1) * rows, lanes] = jnp.concatenate([-low, top], 0).astype(BF16)
            squares = squares + (top * top + low * low)
        power[:, lanes] = jnp.broadcast_to(jnp.sum(squares, axis=0, keepdims=True), (8, mics))
    width = pairs * mics
    first = side * width
    form = (((1,), (1,)), ((), ()))
    step = min(STEP, width)
    for point in range(0, cos_ref.shape[0], LANES):
        rows_now = slice(point, point + LANES)
        y = jnp.zeros((LANES, real_lhs.shape[0]), F32)
        sums = [jnp.zeros((16, LANES), F32)] * (LANES // 16)
        for at in range(0, width, step):
            across = slice(first + at, first + at + step)
            y = y + lax.dot_general(cos_ref[rows_now, across], real_lhs[:, at : at + step], form, preferred_element_type=F32)
            y = y + lax.dot_general(sin_ref[rows_now, across], swap_lhs[:, at : at + step], form, preferred_element_type=F32)
            for lane in range(at, at + step, LANES):
                weight = power[0:1, lane : lane + LANES]
                lanes = slice(first + lane, first + lane + LANES)
                for i in range(LANES // 16):
                    c = cos_ref[point + 16 * i : point + 16 * i + 16, lanes].astype(F32)
                    d = sin_ref[point + 16 * i : point + 16 * i + 16, lanes].astype(F32)
                    sums[i] = sums[i] + (c * c + d * d) * weight
        use(point, y, jnp.concatenate(sums, 0))


def own_kernel(nears, pairs, x_ref, cos_ref, sin_ref, y_ref, diagonal_ref, real_lhs, swap_lhs, power):
    def use(point, y, diagonal):
        y_ref[point : point + LANES, :] = y
        diagonal_ref[point : point + LANES, :] = diagonal

    project(nears, pairs, 0, x_ref, cos_ref, sin_ref, real_lhs, swap_lhs, power, use)


def other_kernel(
    nears, pairs, x_ref, cos_ref, sin_ref, y_ref, diagonal_ref, out_ref, real_lhs, swap_lhs, power
):
    def use(point, y, diagonal):
        y = y + y_ref[point : point + LANES, :]
        value = y * y
        part = value[:, :LANES]
        for lane in range(LANES, value.shape[1], LANES):
            part = part + value[:, lane : lane + LANES]
        part = part - (diagonal + diagonal_ref[point : point + LANES, :])
        line = jnp.sum(part.T, axis=0, keepdims=True)
        at = point // LANES
        out_ref[:, at : at + 1, :] = jnp.broadcast_to(line[None], (out_ref.shape[0], 1, LANES))

    project(nears, pairs, 1, x_ref, cos_ref, sin_ref, real_lhs, swap_lhs, power, use)


def shards(nears, pairs, devices, signal, bins, mic_positions, grid_positions):
    snaps, samples, mics = signal.shape
    total_mics = mic_positions.shape[1]
    points = grid_positions.shape[1]
    half_points = points // 2
    place = jnp.stack([lax.axis_index("near") * pairs + lax.axis_index("pair"), lax.axis_index("core")]).astype(jnp.int32)
    vmem = pl.BlockSpec(memory_space=pltpu.VMEM)
    smem = pl.BlockSpec(memory_space=pltpu.SMEM)
    anywhere = pl.BlockSpec(memory_space=pl.ANY)

    def steer_shape(count):
        return [pltpu.VMEM((count, total_mics), BF16)] * 2

    def in_hbm(array):
        return pltpu.with_memory_space_constraint(array, pltpu.HBM)

    def in_vmem(array):
        return pltpu.with_memory_space_constraint(array, pltpu.VMEM)

    local, cos, sin = pl.pallas_call(
        functools.partial(dft_kernel, pairs),
        in_specs=[smem, anywhere, anywhere, anywhere, anywhere],
        out_specs=[vmem] * 3,
        out_shape=[
            jax.ShapeDtypeStruct((F, 2 * snaps, mics), BF16),
            *steer_shape(half_points),
        ],
        scratch_shapes=[
            pltpu.VMEM((half_points, LANES), BF16),
            pltpu.VMEM((DEPTH, total_mics), BF16),
            pltpu.VMEM((snaps, samples, mics), BF16),
            pltpu.VMEM((2 * F, snaps, mics), F32),
            pltpu.SMEM(bins.shape, jnp.int32),
            pltpu.VMEM(mic_positions.shape, F32),
            pltpu.VMEM(grid_positions.shape, F32),
            pltpu.VMEM((8, total_mics), F32),
            pltpu.SemaphoreType.DMA((3,)),
            pltpu.SemaphoreType.DMA((snaps,)),
        ],
        compiler_params=pltpu.CompilerParams(vmem_limit_bytes=24 * 2**20),
        name="dft_and_steering",
    )(place, in_hbm(bins), in_hbm(mic_positions), in_hbm(grid_positions), in_hbm(signal))
    own = lax.all_to_all(local, ("near", "pair"), 0, 0, tiled=True)
    other = lax.ppermute(own, "core", [(0, 1), (1, 0)])
    wide = -(-nears * 2 * snaps // LANES) * LANES
    side_mics = total_mics // 2
    scratch = [
        pltpu.VMEM((wide, side_mics), BF16),
        pltpu.VMEM((wide, side_mics), BF16),
        pltpu.VMEM((8, side_mics), F32),
    ]
    steer = (in_vmem(cos), in_vmem(sin))
    cost = pl.CostEstimate(
        flops=4 * half_points * wide * side_mics, bytes_accessed=4 * half_points * side_mics, transcendentals=0
    )
    y, diagonal = pl.pallas_call(
        functools.partial(own_kernel, nears, pairs),
        in_specs=[vmem] * 3,
        out_specs=[vmem] * 2,
        out_shape=[pltpu.VMEM((half_points, wide), F32), pltpu.VMEM((half_points, LANES), F32)],
        scratch_shapes=scratch,
        compiler_params=pltpu.CompilerParams(vmem_limit_bytes=8 * 2**20),
        cost_estimate=cost,
        name="own_projection",
    )(own, *steer)
    mine = pl.pallas_call(
        functools.partial(other_kernel, nears, pairs),
        in_specs=[vmem] * 5,
        out_specs=vmem,
        out_shape=jax.ShapeDtypeStruct((devices, half_points // LANES, LANES), F32),
        scratch_shapes=scratch,
        compiler_params=pltpu.CompilerParams(vmem_limit_bytes=8 * 2**20),
        cost_estimate=cost,
        name="other_projection",
    )(other, *steer, in_vmem(y), in_vmem(diagonal))
    axes = ("wide", "near", "pair", "core")
    everyone = lax.all_to_all(mine, axes, 0, 0, tiled=True)
    summed = jnp.sum(everyone.reshape(-1, F, points), axis=0)
    all_snaps = snaps * lax.axis_size("wide") * nears
    return summed * (1.0 / (math.sqrt(all_snaps) * total_mics))


def solution(mesh):
    groups, inner = mesh.shape["grp"], mesh.shape["inner"]
    pairs = inner // 2
    nears = F // pairs
    fine = Mesh(mesh.devices.reshape(groups // nears, nears, pairs, 2), ("wide", "near", "pair", "core"))
    in_specs = (P(("wide", "near"), None, ("pair", "core")), P(), P(), P())
    step = functools.partial(shards, nears, pairs, groups * inner)
    return jax.shard_map(step, mesh=fine, in_specs=in_specs, out_specs=P(), check_vma=False)
```

time: 46.2 us -> 38.9 us (0.84)
  Pallas kernels: 19.6 us -> 14.7 us
  local copies, waits for them, and re-layouts: 2.24 us -> 0.03 us
    pallas_call x3, Pallas kernels: 19.6 us -> 14.7 us  [the longest x1 10.5 us: shards(): pl.pallas_call(functools.partial(dft_kernel, pairs), in_specs=[smem, anyw...]
    unnamed x6 -> x0, local copies, waits for them, and re-layouts: 2.21 us -> none
  transfers between devices with their start and end apart: 1 -> 1, of which waited for: 0 -> 0; matrix products, arithmetic and copies ran while one was open for 0% -> 0% of each run, Pallas kernels for 12% -> 6%
where the time goes in v2:
time: 38.9 us; the launch traced here: 38.8 us
  blocking collectives  23.2 us (60%)
  Pallas kernels  14.7 us (38%)
  other arithmetic  0.7 us (2%)
    all_to_all x1, blocking collectives, shards(): own = lax.all_to_all(local, ('near', 'pair'), 0, 0, tiled=True)  12.6 us
    all_to_all x1, blocking collectives, shards(): everyone = lax.all_to_all(mine, axes, 0, 0, tiled=True)  10.6 us
    pallas_call x1, Pallas kernels, shards(): pl.pallas_call(functools.partial(dft_kernel, pairs), in_specs=[smem, anyw...  10.5 us
    pallas_call x1, Pallas kernels, shards(): pl.pallas_call(functools.partial(other_kernel, nears, pairs), in_specs=[v...  2.14 us
    pallas_call x1, Pallas kernels, shards(): pl.pallas_call(functools.partial(own_kernel, nears, pairs), in_specs=[vme...  2.14 us
  transfers between devices with their start and end apart: 1, of which 0 were waited for; matrix products, arithmetic and copies ran while one was open for 0% of the time, Pallas kernels for 6%

profile of v2, /device:TPU:0, one launch (start us, length us, event | category | flops | bytes accessed | tf_op | source)
XLA Modules:
  0.0 38.8 jit_solution(9864829647087984969)
XLA Ops:
  0.0 0.1 pad_add_fusion.place_ref
  0.1 10.5 %dft_and_steering.1 = (bf16[8,16,1024]{2,1,0:T(8,128)(2,1)S(1)}, bf16[512,4096]{1,0:T(8,128)(2,1)S(1)}, bf16[512,4096]{1,0:T(8,128)(2,1)S(1)}) custom-call(s32[2]{0:T(128)S(1)} %pad_add_fusion.place_ref, s32[8]{0:T(128)} %bins_hbm.1, f32[3,4096]{1,0:T(4,128)} %mic_hbm.1, f32[3,1024]{1,0:T(4,128)} %grid_hbm.1, bf16[8,1024,1024]{2,1,0:T(8,128)(2,1)} %signal_ref.1), custom_call_target="tpu_custom_call" | custom-call | tf_op jit(solution)/shard_map/dft_and_steering/pallas_call | solution.py:248
  10.5 12.6 %all_to_all.10.x_ref = bf16[8,16,1024]{2,1,0:T(8,128)(2,1)S(1)} all-to-all(bf16[8,16,1024]{2,1,0:T(8,128)(2,1)S(1)} %get-tuple-element.10), channel_id=1, replica_groups=mesh['wide'=2,'near'=4,'pair'=2,'core'=2] {'near','pair'}, dimensions={0} | all-to-all | bytes 524288 | tf_op jit(solution)/shard_map/all_to_all | solution.py:271
  23.1 0.0 collective-permute-start
  23.2 2.1 %own_projection.1 = (f32[512,128]{1,0:T(8,128)S(1)}, f32[512,128]{1,0:T(8,128)S(1)}) custom-call(bf16[8,16,1024]{2,1,0:T(8,128)(2,1)S(1)} %all_to_all.10.x_ref, bf16[512,4096]{1,0:T(8,128)(2,1)S(1)} %get-tuple-element.11.cos_ref, bf16[512,4096]{1,0:T(8,128)(2,1)S(1)} %get-tuple-element.12.sin_ref), custom_call_target="tpu_custom_call" | custom-call | flops 536870912 | bytes 4194304 | tf_op jit(solution)/shard_map/own_projection/pallas_call | solution.py:284
  25.3 0.0 collective-permute-done.x_ref
  25.3 2.1 %other_projection.1 = f32[32,4,128]{2,1,0:T(4,128)S(1)} custom-call(bf16[8,16,1024]{2,1,0:T(8,128)(2,1)S(1)} %collective-permute-done.x_ref, bf16[512,4096]{1,0:T(8,128)(2,1)S(1)} %get-tuple-element.11.cos_ref, bf16[512,4096]{1,0:T(8,128)(2,1)S(1)} %get-tuple-element.12.sin_ref, f32[512,128]{1,0:T(8,128)S(1)} %get-tuple-element.13.y_ref, ...), custom_call_target="tpu_custom_call" | custom-call | flops 536870912 | bytes 4194304 | tf_op jit(solution)/shard_map/other_projection/pallas_call | solution.py:294
  27.5 10.6 %all_to_all.11 = f32[32,4,128]{2,1,0:T(4,128)S(1)} all-to-all(f32[32,4,128]{2,1,0:T(4,128)S(1)} %other_projection.1), channel_id=1, replica_groups=mesh['wide'=2,'near'=4,'pair'=2,'core'=2] {'wide','near','pair','core'}, dimensions={0} | all-to-all | bytes 131072 | tf_op jit(solution)/shard_map/all_to_all | solution.py:305
  38.1 0.6 %broadcast_multiply_fusion = f32[8,1024]{1,0:T(8,128)} fusion(f32[8,1024]{1,0:T(8,128)S(1)} %reduce_sum.9), kind=kLoop, calls=%fused_computation | loop fusion | flops 8192 | bytes 65536 | tf_op jit(solution)/shard_map/mul | solution.py:308
  (2 shorter events, 0.0 us)
Async XLA Ops:
  23.1 2.2 %collective-permute-start = (bf16[8,16,1024]{2,1,0:T(8,128)(2,1)S(1)}, bf16[8,16,1024]{2,1,0:T(8,128)(2,1)S(1)}, u32[]{:S(2)}, u32[]{:S(2)}) collective-permute-start(bf16[8,16,1024]{2,1,0:T(8,128)(2,1)S(1)} %all_to_all.10.x_ref), channel_id=1, source_target_pairs={{0,1},{1,0},{2,3},{3,2},{4,5},{5,4},{6,7},{7,6},{8,9},{9,8},{10,11... | collective-permute-start | bytes 786440 | tf_op jit(solution)/shard_map/ppermute | solution.py:272

commit v3 on v2

--- a/solution.py
+++ b/solution.py
@@ -19,7 +19,7 @@
 STEP = 512
 COLUMNS = 256
 
-SIN_HALF = (4.4428679027342115, -7.307443409650812, 3.5947879684072226, -0.7843737403612829)
+SIN_HALF = (4.441535724093539, -7.264680926673255, 3.25204996020452)
 COS_HALF = (1.414204080247352, -6.9776420363098905, 5.715238127798347, -1.7283478206531864)
 SIN_FINE = (4.442882937668975, -7.308249445082402, 3.6064748105185624, -0.8474638068718637, 0.11600967661123661, -0.009900200019037797)
 COS_FINE = (1.4142135623720369, -6.978864199223495, 5.739885708320473, -1.8883460768140574, 0.33280043358005373, -0.036453250292718266, 0.0026021832760962107)
@@ -37,7 +37,7 @@
     u = r * r
     s = polynomial(sin_half, u) * r
     c = polynomial(cos_half, u)
-    return 1.0 - s * s, s * c
+    return c * c - 1.0, s * c
 
 
 def dft_table(bins_ref, samples):
@@ -90,15 +90,24 @@
     left_ref[...] = jnp.concatenate(groups + [zeros], 0).T.astype(BF16)
 
 
-def steer_rows(row, out_row, count, lanes, left_ref, right_ref, cos_ref, sin_ref):
-    left = left_ref[pl.ds(row, count), 0:DEPTH]
-    out_rows = pl.ds(out_row, count)
-    step = lanes.step
-    for at in lanes:
-        square = jnp.dot(left, right_ref[0:DEPTH, at : at + step], preferred_element_type=F32)
-        cos, sin = cos_sin(square * lax.rsqrt(square))
-        cos_ref[out_rows, at : at + step] = cos.astype(BF16)
-        sin_ref[out_rows, at : at + step] = sin.astype(BF16)
+def steer_block(row, row_end, at, width, left_ref, right_ref, cos_ref, sin_ref):
+    lanes = slice(at, at + width)
+    square = jnp.dot(left_ref[row:row_end, 0:DEPTH], right_ref[0:DEPTH, lanes], preferred_element_type=F32)
+    cos, sin = cos_sin(square * lax.rsqrt(square))
+    cos_ref[row:row_end, lanes] = cos.astype(BF16)
+    sin_ref[row:row_end, lanes] = sin.astype(BF16)
+
+
+def stages(snaps, points):
+    first = max(points * 5 // 16 // 16 * 16, 16)
+    second = first + (points - first) // 32 * 16
+    return [(0, first), (snaps // 2, second), (snaps, points)]
+
+
+def interleaved(left, right):
+    count = max(len(left), len(right))
+    for i in range(count):
+        yield tuple(work[i * len(work) // count : (i + 1) * len(work) // count] for work in (left, right))
 
 
 def mic_order(pairs, width, core):
@@ -130,44 +139,33 @@
     order = mic_order(pairs, mics, core)
     distance_factors(scale, mic_ref, order, grid_ref, core * (grid_ref.shape[1] // 2), rows8, left_ref, right_ref)
     table = dft_table(bins_ref, samples)
-    each = cos_ref.shape[0] // snaps
-    parts = max(mics // COLUMNS, 1)
-    columns = mics // parts
-    width = right_ref.shape[1] // parts
-
-    def steer(s, part):
-        row = pl.multiple_of(s * each, 16)
-        lanes = range(part * width, (part + 1) * width, min(STEP, width))
-        steer_rows(row, row, each, lanes, left_ref, right_ref, cos_ref, sin_ref)
-
-    def transform(s, part):
-        across = slice(part * columns, (part + 1) * columns)
-        total[:, pl.ds(s, 1), across] = jnp.dot(table, held[s, :, across], preferred_element_type=F32)[:, None, :]
-
-    def step(s, carry):
-        copy(s).wait()
-        for part in range(parts):
-            transform(s, part)
-            steer(s + 1, part)
-        return carry
-
-    for part in range(parts):
-        steer(0, part)
-    lax.fori_loop(0, snaps - 1, step, 0)
-    copy(snaps - 1).wait()
-    for part in range(parts):
-        transform(snaps - 1, part)
+
+    def transform(s, at, width):
+        across = slice(at, at + width)
+        total[:, s : s + 1, across] = jnp.dot(table, held[s, :, across], preferred_element_type=F32)[:, None, :]
+
+    columns = min(COLUMNS, mics)
+    points, lanes = cos_ref.shape
+    step = min(STEP, lanes)
+    row = snap = 0
+    for snap_end, row_end in stages(snaps, points):
+        for s in range(snap, snap_end):
+            copy(s).wait()
+        transforms = [(s, at, columns) for s in range(snap, snap_end) for at in range(0, mics, columns)]
+        steerings = [(row, row_end, at, step) for at in range(0, lanes, step)]
+        for take_transforms, take_steerings in interleaved(transforms, steerings):
+            for args in take_transforms:
+                transform(*args)
+            for args in take_steerings:
+                steer_block(*args, left_ref, right_ref, cos_ref, sin_ref)
+        row, snap = row_end, snap_end
     for f in range(F):
         out_ref[f] = jnp.concatenate([total[f], total[F + f]], 0).astype(BF16)
 
 
-def project(nears, pairs, side, x_ref, cos_ref, sin_ref, real_lhs, swap_lhs, power, use):
+def project(nears, pairs, side, x_ref, cos_ref, sin_ref, real_lhs, swap_lhs, power):
     blocks, rows, mics = x_ref.shape
     half = rows // 2
-    used = nears * rows
-    if used < real_lhs.shape[0]:
-        real_lhs[used:, :] = jnp.zeros((real_lhs.shape[0] - used, real_lhs.shape[1]), BF16)
-        swap_lhs[used:, :] = jnp.zeros((real_lhs.shape[0] - used, real_lhs.shape[1]), BF16)
     for pair in range(pairs):
         lanes = slice(pair * mics, (pair + 1) * mics)
         squares = jnp.zeros((half, mics), F32)
@@ -183,47 +181,38 @@
     first = side * width
     form = (((1,), (1,)), ((), ()))
     step = min(STEP, width)
-    for point in range(0, cos_ref.shape[0], LANES):
-        rows_now = slice(point, point + LANES)
-        y = jnp.zeros((LANES, real_lhs.shape[0]), F32)
-        sums = [jnp.zeros((16, LANES), F32)] * (LANES // 16)
-        for at in range(0, width, step):
-            across = slice(first + at, first + at + step)
-            y = y + lax.dot_general(cos_ref[rows_now, across], real_lhs[:, at : at + step], form, preferred_element_type=F32)
-            y = y + lax.dot_general(sin_ref[rows_now, across], swap_lhs[:, at : at + step], form, preferred_element_type=F32)
+    points = cos_ref.shape[0]
+    y = jnp.zeros((points, real_lhs.shape[0]), F32)
+    sums = [jnp.zeros((16, LANES), F32)] * (points // 16)
+    for at in range(0, width, step):
+        across = slice(first + at, first + at + step)
+        y = y + lax.dot_general(cos_ref[:, across], real_lhs[:, at : at + step], form, preferred_element_type=F32)
+        y = y + lax.dot_general(sin_ref[:, across], swap_lhs[:, at : at + step], form, preferred_element_type=F32)
+        for i in range(points // 16):
             for lane in range(at, at + step, LANES):
                 weight = power[0:1, lane : lane + LANES]
                 lanes = slice(first + lane, first + lane + LANES)
-                for i in range(LANES // 16):
-                    c = cos_ref[point + 16 * i : point + 16 * i + 16, lanes].astype(F32)
-                    d = sin_ref[point + 16 * i : point + 16 * i + 16, lanes].astype(F32)
-                    sums[i] = sums[i] + (c * c + d * d) * weight
-        use(point, y, jnp.concatenate(sums, 0))
+                c = cos_ref[16 * i : 16 * i + 16, lanes].astype(F32)
+                d = sin_ref[16 * i : 16 * i + 16, lanes].astype(F32)
+                sums[i] = sums[i] + (c * c + d * d) * weight
+    return y, jnp.concatenate(sums, 0)
 
 
 def own_kernel(nears, pairs, x_ref, cos_ref, sin_ref, y_ref, diagonal_ref, real_lhs, swap_lhs, power):
-    def use(point, y, diagonal):
-        y_ref[point : point + LANES, :] = y
-        diagonal_ref[point : point + LANES, :] = diagonal
-
-    project(nears, pairs, 0, x_ref, cos_ref, sin_ref, real_lhs, swap_lhs, power, use)
+    y_ref[...], diagonal_ref[...] = project(nears, pairs, 0, x_ref, cos_ref, sin_ref, real_lhs, swap_lhs, power)
 
 
 def other_kernel(
     nears, pairs, x_ref, cos_ref, sin_ref, y_ref, diagonal_ref, out_ref, real_lhs, swap_lhs, power
 ):
-    def use(point, y, diagonal):
-        y = y + y_ref[point : point + LANES, :]
-        value = y * y
-        part = value[:, :LANES]
-        for lane in range(LANES, value.shape[1], LANES):
-            part = part + value[:, lane : lane + LANES]
-        part = part - (diagonal + diagonal_ref[point : point + LANES, :])
-        line = jnp.sum(part.T, axis=0, keepdims=True)
-        at = point // LANES
-        out_ref[:, at : at + 1, :] = jnp.broadcast_to(line[None], (out_ref.shape[0], 1, LANES))
-
-    project(nears, pairs, 1, x_ref, cos_ref, sin_ref, real_lhs, swap_lhs, power, use)
+    y, diagonal = project(nears, pairs, 1, x_ref, cos_ref, sin_ref, real_lhs, swap_lhs, power)
+    y = y + y_ref[...]
+    value = y * y
+    diagonal = diagonal + diagonal_ref[...]
+    for block in range(out_ref.shape[1]):
+        rows = slice(block * LANES, (block + 1) * LANES)
+        line = jnp.sum(value[rows].T, axis=0, keepdims=True) - jnp.sum(diagonal[rows].T, axis=0, keepdims=True)
+        out_ref[:, block : block + 1, :] = jnp.broadcast_to(line[None], (out_ref.shape[0], 1, LANES))
 
 
 def shards(nears, pairs, devices, signal, bins, mic_positions, grid_positions):
@@ -270,7 +259,7 @@
     )(place, in_hbm(bins), in_hbm(mic_positions), in_hbm(grid_positions), in_hbm(signal))
     own = lax.all_to_all(local, ("near", "pair"), 0, 0, tiled=True)
     other = lax.ppermute(own, "core", [(0, 1), (1, 0)])
-    wide = -(-nears * 2 * snaps // LANES) * LANES
+    wide = nears * 2 * snaps
     side_mics = total_mics // 2
     scratch = [
         pltpu.VMEM((wide, side_mics), BF16),

time: 38.9 us -> 38 us (0.977)
  Pallas kernels: 14.7 us -> 13.8 us
    pallas_call x1, Pallas kernels: 10.5 us -> 9.74 us  [shards(): pl.pallas_call(functools.partial(dft_kernel, pairs), in_specs=[smem, anyw...]
  transfers between devices with their start and end apart: 1 -> 1, of which waited for: 0 -> 0; matrix products, arithmetic and copies ran while one was open for 0% -> 0% of each run, Pallas kernels for 6% -> 5%
where the time goes in v3:
time: 38 us; the launch traced here: 37.8 us
  blocking collectives  23.2 us (61%)
  Pallas kernels  13.8 us (36%)
  other arithmetic  0.7 us (2%)
    all_to_all x1, blocking collectives, shards(): own = lax.all_to_all(local, ('near', 'pair'), 0, 0, tiled=True)  12.6 us
    all_to_all x1, blocking collectives, shards(): everyone = lax.all_to_all(mine, axes, 0, 0, tiled=True)  10.6 us
    pallas_call x1, Pallas kernels, shards(): pl.pallas_call(functools.partial(dft_kernel, pairs), in_specs=[smem, anyw...  9.74 us
    pallas_call x1, Pallas kernels, shards(): pl.pallas_call(functools.partial(other_kernel, nears, pairs), in_specs=[v...  2.19 us
    pallas_call x1, Pallas kernels, shards(): pl.pallas_call(functools.partial(own_kernel, nears, pairs), in_specs=[vme...  1.89 us
  transfers between devices with their start and end apart: 1, of which 0 were waited for; matrix products, arithmetic and copies ran while one was open for 0% of the time, Pallas kernels for 5%

profile of v3, /device:TPU:0, one launch (start us, length us, event | category | flops | bytes accessed | tf_op | source)
XLA Modules:
  0.0 37.8 jit_solution(14740840738436840374)
XLA Ops:
  0.0 0.1 pad_add_fusion.place_ref
  0.1 9.7 %dft_and_steering.1 = (bf16[8,16,1024]{2,1,0:T(8,128)(2,1)S(1)}, bf16[512,4096]{1,0:T(8,128)(2,1)S(1)}, bf16[512,4096]{1,0:T(8,128)(2,1)S(1)}) custom-call(s32[2]{0:T(128)S(1)} %pad_add_fusion.place_ref, s32[8]{0:T(128)} %bins_hbm.1, f32[3,4096]{1,0:T(4,128)} %mic_hbm.1, f32[3,1024]{1,0:T(4,128)} %grid_hbm.1, bf16[8,1024,1024]{2,1,0:T(8,128)(2,1)} %signal_ref.1), custom_call_target="tpu_custom_call" | custom-call | tf_op jit(solution)/shard_map/dft_and_steering/pallas_call | solution.py:237
  9.8 12.6 %all_to_all.10.x_ref = bf16[8,16,1024]{2,1,0:T(8,128)(2,1)S(1)} all-to-all(bf16[8,16,1024]{2,1,0:T(8,128)(2,1)S(1)} %get-tuple-element.10), channel_id=1, replica_groups=mesh['wide'=2,'near'=4,'pair'=2,'core'=2] {'near','pair'}, dimensions={0} | all-to-all | bytes 524288 | tf_op jit(solution)/shard_map/all_to_all | solution.py:260
  22.4 0.0 collective-permute-start
  22.4 1.9 %own_projection.1 = (f32[512,64]{1,0:T(8,128)S(1)}, f32[512,128]{1,0:T(8,128)S(1)}) custom-call(bf16[8,16,1024]{2,1,0:T(8,128)(2,1)S(1)} %all_to_all.10.x_ref, bf16[512,4096]{1,0:T(8,128)(2,1)S(1)} %get-tuple-element.11.cos_ref, bf16[512,4096]{1,0:T(8,128)(2,1)S(1)} %get-tuple-element.12.sin_ref), custom_call_target="tpu_custom_call" | custom-call | flops 268435456 | bytes 4194304 | tf_op jit(solution)/shard_map/own_projection/pallas_call | solution.py:273
  24.3 0.0 collective-permute-done.x_ref
  24.3 2.2 %other_projection.1 = f32[32,4,128]{2,1,0:T(4,128)S(1)} custom-call(bf16[8,16,1024]{2,1,0:T(8,128)(2,1)S(1)} %collective-permute-done.x_ref, bf16[512,4096]{1,0:T(8,128)(2,1)S(1)} %get-tuple-element.11.cos_ref, bf16[512,4096]{1,0:T(8,128)(2,1)S(1)} %get-tuple-element.12.sin_ref, f32[512,64]{1,0:T(8,128)S(1)} %get-tuple-element.13.y_ref, ...), custom_call_target="tpu_custom_call" | custom-call | flops 268435456 | bytes 4194304 | tf_op jit(solution)/shard_map/other_projection/pallas_call | solution.py:283
  26.5 10.6 %all_to_all.11 = f32[32,4,128]{2,1,0:T(4,128)S(1)} all-to-all(f32[32,4,128]{2,1,0:T(4,128)S(1)} %other_projection.1), channel_id=1, replica_groups=mesh['wide'=2,'near'=4,'pair'=2,'core'=2] {'wide','near','pair','core'}, dimensions={0} | all-to-all | bytes 131072 | tf_op jit(solution)/shard_map/all_to_all | solution.py:294
  37.2 0.6 %broadcast_multiply_fusion = f32[8,1024]{1,0:T(8,128)} fusion(f32[8,1024]{1,0:T(8,128)S(1)} %reduce_sum.9), kind=kLoop, calls=%fused_computation | loop fusion | flops 8192 | bytes 65536 | tf_op jit(solution)/shard_map/mul | solution.py:297
  (2 shorter events, 0.0 us)
Async XLA Ops:
  22.4 1.9 %collective-permute-start = (bf16[8,16,1024]{2,1,0:T(8,128)(2,1)S(1)}, bf16[8,16,1024]{2,1,0:T(8,128)(2,1)S(1)}, u32[]{:S(2)}, u32[]{:S(2)}) collective-permute-start(bf16[8,16,1024]{2,1,0:T(8,128)(2,1)S(1)} %all_to_all.10.x_ref), channel_id=1, source_target_pairs={{0,1},{1,0},{2,3},{3,2},{4,5},{5,4},{6,7},{7,6},{8,9},{9,8},{10,11... | collective-permute-start | bytes 786440 | tf_op jit(solution)/shard_map/ppermute | solution.py:261

commit v4 on v3

--- a/solution.py
+++ b/solution.py
@@ -180,22 +180,22 @@
     width = pairs * mics
     first = side * width
     form = (((1,), (1,)), ((), ()))
-    step = min(STEP, width)
+    step = min(COLUMNS, width)
     points = cos_ref.shape[0]
     y = jnp.zeros((points, real_lhs.shape[0]), F32)
-    sums = [jnp.zeros((16, LANES), F32)] * (points // 16)
+    diagonal = jnp.zeros((points, LANES), F32)
     for at in range(0, width, step):
-        across = slice(first + at, first + at + step)
-        y = y + lax.dot_general(cos_ref[:, across], real_lhs[:, at : at + step], form, preferred_element_type=F32)
-        y = y + lax.dot_general(sin_ref[:, across], swap_lhs[:, at : at + step], form, preferred_element_type=F32)
-        for i in range(points // 16):
-            for lane in range(at, at + step, LANES):
-                weight = power[0:1, lane : lane + LANES]
-                lanes = slice(first + lane, first + lane + LANES)
-                c = cos_ref[16 * i : 16 * i + 16, lanes].astype(F32)
-                d = sin_ref[16 * i : 16 * i + 16, lanes].astype(F32)
-                sums[i] = sums[i] + (c * c + d * d) * weight
-    return y, jnp.concatenate(sums, 0)
+        here = slice(at, at + step)
+        cos = cos_ref[:, first + at : first + at + step]
+        sin = sin_ref[:, first + at : first + at + step]
+        y = y + lax.dot_general(cos, real_lhs[:, here], form, preferred_element_type=F32)
+        y = y + lax.dot_general(sin, swap_lhs[:, here], form, preferred_element_type=F32)
+        cos = cos.astype(F32)
+        sin = sin.astype(F32)
+        weighted = (cos * cos + sin * sin) * power[0:1, here]
+        for lane in range(0, step, LANES):
+            diagonal = diagonal + weighted[:, lane : lane + LANES]
+    return y, diagonal
 
 
 def own_kernel(nears, pairs, x_ref, cos_ref, sin_ref, y_ref, diagonal_ref, real_lhs, swap_lhs, power):

time: 38 us -> 37 us (0.974)
  Pallas kernels: 13.8 us -> 12.8 us
    pallas_call x1, Pallas kernels: 2.19 us -> 1.61 us  [shards(): pl.pallas_call(functools.partial(other_kernel, nears, pairs), in_specs=[v...]
    pallas_call x1, Pallas kernels: 1.89 us -> 1.47 us  [shards(): pl.pallas_call(functools.partial(own_kernel, nears, pairs), in_specs=[vme...]
  transfers between devices with their start and end apart: 1 -> 1, of which waited for: 0 -> 1; matrix products, arithmetic and copies ran while one was open for 0% -> 0% of each run, Pallas kernels for 5% -> 4%
where the time goes in v4:
time: 37 us; the launch traced here: 36.8 us
  blocking collectives  23.2 us (63%)
  Pallas kernels  12.8 us (35%)
  other arithmetic  0.7 us (2%)
    all_to_all x1, blocking collectives, shards(): own = lax.all_to_all(local, ('near', 'pair'), 0, 0, tiled=True)  12.6 us
    all_to_all x1, blocking collectives, shards(): everyone = lax.all_to_all(mine, axes, 0, 0, tiled=True)  10.6 us
    pallas_call x1, Pallas kernels, shards(): pl.pallas_call(functools.partial(dft_kernel, pairs), in_specs=[smem, anyw...  9.74 us
    pallas_call x1, Pallas kernels, shards(): pl.pallas_call(functools.partial(other_kernel, nears, pairs), in_specs=[v...  1.61 us
    pallas_call x1, Pallas kernels, shards(): pl.pallas_call(functools.partial(own_kernel, nears, pairs), in_specs=[vme...  1.47 us
  transfers between devices with their start and end apart: 1, of which 1 were waited for; matrix products, arithmetic and copies ran while one was open for 0% of the time, Pallas kernels for 4%

profile of v4, /device:TPU:0, one launch (start us, length us, event | category | flops | bytes accessed | tf_op | source)
XLA Modules:
  0.0 36.8 jit_solution(12644716382210308013)
XLA Ops:
  0.0 0.1 pad_add_fusion.place_ref
  0.1 9.7 %dft_and_steering.1 = (bf16[8,16,1024]{2,1,0:T(8,128)(2,1)S(1)}, bf16[512,4096]{1,0:T(8,128)(2,1)S(1)}, bf16[512,4096]{1,0:T(8,128)(2,1)S(1)}) custom-call(s32[2]{0:T(128)S(1)} %pad_add_fusion.place_ref, s32[8]{0:T(128)} %bins_hbm.1, f32[3,4096]{1,0:T(4,128)} %mic_hbm.1, f32[3,1024]{1,0:T(4,128)} %grid_hbm.1, bf16[8,1024,1024]{2,1,0:T(8,128)(2,1)} %signal_ref.1), custom_call_target="tpu_custom_call" | custom-call | tf_op jit(solution)/shard_map/dft_and_steering/pallas_call | solution.py:237
  9.8 12.6 %all_to_all.10.x_ref = bf16[8,16,1024]{2,1,0:T(8,128)(2,1)S(1)} all-to-all(bf16[8,16,1024]{2,1,0:T(8,128)(2,1)S(1)} %get-tuple-element.10), channel_id=1, replica_groups=mesh['wide'=2,'near'=4,'pair'=2,'core'=2] {'near','pair'}, dimensions={0} | all-to-all | bytes 524288 | tf_op jit(solution)/shard_map/all_to_all | solution.py:260
  22.4 0.0 collective-permute-start
  22.4 1.5 %own_projection.1 = (f32[512,64]{1,0:T(8,128)S(1)}, f32[512,128]{1,0:T(8,128)S(1)}) custom-call(bf16[8,16,1024]{2,1,0:T(8,128)(2,1)S(1)} %all_to_all.10.x_ref, bf16[512,4096]{1,0:T(8,128)(2,1)S(1)} %get-tuple-element.11.cos_ref, bf16[512,4096]{1,0:T(8,128)(2,1)S(1)} %get-tuple-element.12.sin_ref), custom_call_target="tpu_custom_call" | custom-call | flops 268435456 | bytes 4194304 | tf_op jit(solution)/shard_map/own_projection/pallas_call | solution.py:273
  23.9 0.1 collective-permute-done.x_ref
  24.0 1.6 %other_projection.1 = f32[32,4,128]{2,1,0:T(4,128)S(1)} custom-call(bf16[8,16,1024]{2,1,0:T(8,128)(2,1)S(1)} %collective-permute-done.x_ref, bf16[512,4096]{1,0:T(8,128)(2,1)S(1)} %get-tuple-element.11.cos_ref, bf16[512,4096]{1,0:T(8,128)(2,1)S(1)} %get-tuple-element.12.sin_ref, f32[512,64]{1,0:T(8,128)S(1)} %get-tuple-element.13.y_ref, ...), custom_call_target="tpu_custom_call" | custom-call | flops 268435456 | bytes 4194304 | tf_op jit(solution)/shard_map/other_projection/pallas_call | solution.py:283
  25.6 10.6 %all_to_all.11 = f32[32,4,128]{2,1,0:T(4,128)S(1)} all-to-all(f32[32,4,128]{2,1,0:T(4,128)S(1)} %other_projection.1), channel_id=1, replica_groups=mesh['wide'=2,'near'=4,'pair'=2,'core'=2] {'wide','near','pair','core'}, dimensions={0} | all-to-all | bytes 131072 | tf_op jit(solution)/shard_map/all_to_all | solution.py:294
  36.2 0.6 %broadcast_multiply_fusion = f32[8,1024]{1,0:T(8,128)} fusion(f32[8,1024]{1,0:T(8,128)S(1)} %reduce_sum.9), kind=kLoop, calls=%fused_computation | loop fusion | flops 8192 | bytes 65536 | tf_op jit(solution)/shard_map/mul | solution.py:297
  (2 shorter events, 0.0 us)
Async XLA Ops:
  22.4 1.5 %collective-permute-start = (bf16[8,16,1024]{2,1,0:T(8,128)(2,1)S(1)}, bf16[8,16,1024]{2,1,0:T(8,128)(2,1)S(1)}, u32[]{:S(2)}, u32[]{:S(2)}) collective-permute-start(bf16[8,16,1024]{2,1,0:T(8,128)(2,1)S(1)} %all_to_all.10.x_ref), channel_id=1, source_target_pairs={{0,1},{1,0},{2,3},{3,2},{4,5},{5,4},{6,7},{7,6},{8,9},{9,8},{10,11... | collective-permute-start | bytes 786440 | tf_op jit(solution)/shard_map/ppermute | solution.py:261

commit v5 on v4

--- a/solution.py
+++ b/solution.py
@@ -13,7 +13,6 @@
 RATE_OVER_SOUND = 51200.0 / 343.0
 F32 = jnp.float32
 BF16 = jnp.bfloat16
-ROUNDER = 12582912.0
 LANES = 128
 DEPTH = 64
 STEP = 512
@@ -33,7 +32,7 @@
 
 
 def cos_sin(turns, sin_half=SIN_HALF, cos_half=COS_HALF):
-    r = turns - ((turns + ROUNDER) - ROUNDER)
+    r = turns - jnp.round(turns)
     u = r * r
     s = polynomial(sin_half, u) * r
     c = polynomial(cos_half, u)
@@ -49,7 +48,7 @@
         bins = jnp.where(row == f, bins_ref[f], bins)
     turns = ((bins * ticks) & (samples - 1)).astype(F32) * (1.0 / samples)
     half = ticks.astype(F32) * (1.0 / samples)
-    half = half - ((half + ROUNDER) - ROUNDER)
+    half = half - jnp.round(half)
     half_sin = polynomial(SIN_FINE, half * half) * half
     window = 0.5 * half_sin * half_sin * math.sqrt(8.0 / (3.0 * samples))
     cos, sin = cos_sin(turns, SIN_FINE, COS_FINE)
@@ -99,9 +98,12 @@
 
 
 def stages(snaps, points):
-    first = max(points * 5 // 16 // 16 * 16, 16)
-    second = first + (points - first) // 32 * 16
-    return [(0, first), (snaps // 2, second), (snaps, points)]
+    count = 4
+    first = points // 4
+    yield 0, first
+    for stage in range(1, count + 1):
+        row_end = first + (points - first) // 16 * stage // count * 16
+        yield snaps * stage // count, points if stage == count else row_end
 
 
 def interleaved(left, right):

time: 37 us -> 36.1 us (0.976)
  Pallas kernels: 12.8 us -> 12 us
    pallas_call x1, Pallas kernels: 9.74 us -> 8.87 us  [shards(): pl.pallas_call(functools.partial(dft_kernel, pairs), in_specs=[smem, anyw...]
where the time goes in v5:
time: 36.1 us; the launch traced here: 36 us
  blocking collectives  23.2 us (64%)
  Pallas kernels  12 us (33%)
  other arithmetic  0.7 us (2%)
    all_to_all x1, blocking collectives, shards(): own = lax.all_to_all(local, ('near', 'pair'), 0, 0, tiled=True)  12.6 us
    all_to_all x1, blocking collectives, shards(): everyone = lax.all_to_all(mine, axes, 0, 0, tiled=True)  10.6 us
    pallas_call x1, Pallas kernels, shards(): pl.pallas_call(functools.partial(dft_kernel, pairs), in_specs=[smem, anyw...  8.87 us
    pallas_call x1, Pallas kernels, shards(): pl.pallas_call(functools.partial(other_kernel, nears, pairs), in_specs=[v...  1.61 us
    pallas_call x1, Pallas kernels, shards(): pl.pallas_call(functools.partial(own_kernel, nears, pairs), in_specs=[vme...  1.47 us
  transfers between devices with their start and end apart: 1, of which 1 were waited for; matrix products, arithmetic and copies ran while one was open for 0% of the time, Pallas kernels for 4%

profile of v5, /device:TPU:0, one launch (start us, length us, event | category | flops | bytes accessed | tf_op | source)
XLA Modules:
  0.0 36.0 jit_solution(16701112029443088019)
XLA Ops:
  0.0 0.1 pad_add_fusion.place_ref
  0.1 8.9 %dft_and_steering.1 = (bf16[8,16,1024]{2,1,0:T(8,128)(2,1)S(1)}, bf16[512,4096]{1,0:T(8,128)(2,1)S(1)}, bf16[512,4096]{1,0:T(8,128)(2,1)S(1)}) custom-call(s32[2]{0:T(128)S(1)} %pad_add_fusion.place_ref, s32[8]{0:T(128)} %bins_hbm.1, f32[3,4096]{1,0:T(4,128)} %mic_hbm.1, f32[3,1024]{1,0:T(4,128)} %grid_hbm.1, bf16[8,1024,1024]{2,1,0:T(8,128)(2,1)} %signal_ref.1), custom_call_target="tpu_custom_call" | custom-call | tf_op jit(solution)/shard_map/dft_and_steering/pallas_call | solution.py:239
  9.0 12.6 %all_to_all.10.x_ref = bf16[8,16,1024]{2,1,0:T(8,128)(2,1)S(1)} all-to-all(bf16[8,16,1024]{2,1,0:T(8,128)(2,1)S(1)} %get-tuple-element.10), channel_id=1, replica_groups=mesh['wide'=2,'near'=4,'pair'=2,'core'=2] {'near','pair'}, dimensions={0} | all-to-all | bytes 524288 | tf_op jit(solution)/shard_map/all_to_all | solution.py:262
  21.6 0.0 collective-permute-start
  21.6 1.5 %own_projection.1 = (f32[512,64]{1,0:T(8,128)S(1)}, f32[512,128]{1,0:T(8,128)S(1)}) custom-call(bf16[8,16,1024]{2,1,0:T(8,128)(2,1)S(1)} %all_to_all.10.x_ref, bf16[512,4096]{1,0:T(8,128)(2,1)S(1)} %get-tuple-element.11.cos_ref, bf16[512,4096]{1,0:T(8,128)(2,1)S(1)} %get-tuple-element.12.sin_ref), custom_call_target="tpu_custom_call" | custom-call | flops 268435456 | bytes 4194304 | tf_op jit(solution)/shard_map/own_projection/pallas_call | solution.py:275
  23.0 0.1 collective-permute-done.x_ref
  23.1 1.6 %other_projection.1 = f32[32,4,128]{2,1,0:T(4,128)S(1)} custom-call(bf16[8,16,1024]{2,1,0:T(8,128)(2,1)S(1)} %collective-permute-done.x_ref, bf16[512,4096]{1,0:T(8,128)(2,1)S(1)} %get-tuple-element.11.cos_ref, bf16[512,4096]{1,0:T(8,128)(2,1)S(1)} %get-tuple-element.12.sin_ref, f32[512,64]{1,0:T(8,128)S(1)} %get-tuple-element.13.y_ref, ...), custom_call_target="tpu_custom_call" | custom-call | flops 268435456 | bytes 4194304 | tf_op jit(solution)/shard_map/other_projection/pallas_call | solution.py:285
  24.7 10.6 %all_to_all.11 = f32[32,4,128]{2,1,0:T(4,128)S(1)} all-to-all(f32[32,4,128]{2,1,0:T(4,128)S(1)} %other_projection.1), channel_id=1, replica_groups=mesh['wide'=2,'near'=4,'pair'=2,'core'=2] {'wide','near','pair','core'}, dimensions={0} | all-to-all | bytes 131072 | tf_op jit(solution)/shard_map/all_to_all | solution.py:296
  35.3 0.6 %broadcast_multiply_fusion = f32[8,1024]{1,0:T(8,128)} fusion(f32[8,1024]{1,0:T(8,128)S(1)} %reduce_sum.9), kind=kLoop, calls=%fused_computation | loop fusion | flops 8192 | bytes 65536 | tf_op jit(solution)/shard_map/mul | solution.py:299
  (2 shorter events, 0.0 us)
Async XLA Ops:
  21.6 1.5 %collective-permute-start = (bf16[8,16,1024]{2,1,0:T(8,128)(2,1)S(1)}, bf16[8,16,1024]{2,1,0:T(8,128)(2,1)S(1)}, u32[]{:S(2)}, u32[]{:S(2)}) collective-permute-start(bf16[8,16,1024]{2,1,0:T(8,128)(2,1)S(1)} %all_to_all.10.x_ref), channel_id=1, source_target_pairs={{0,1},{1,0},{2,3},{3,2},{4,5},{5,4},{6,7},{7,6},{8,9},{9,8},{10,11... | collective-permute-start | bytes 786440 | tf_op jit(solution)/shard_map/ppermute | solution.py:263

commit v6 on v5

--- a/solution.py
+++ b/solution.py
@@ -144,7 +144,7 @@
 
     def transform(s, at, width):
         across = slice(at, at + width)
-        total[:, s : s + 1, across] = jnp.dot(table, held[s, :, across], preferred_element_type=F32)[:, None, :]
+        total[s, :, across] = jnp.dot(table, held[s, :, across], preferred_element_type=F32)
 
     columns = min(COLUMNS, mics)
     points, lanes = cos_ref.shape
@@ -161,8 +161,11 @@
             for args in take_steerings:
                 steer_block(*args, left_ref, right_ref, cos_ref, sin_ref)
         row, snap = row_end, snap_end
-    for f in range(F):
-        out_ref[f] = jnp.concatenate([total[f], total[F + f]], 0).astype(BF16)
+    for at in range(0, mics, columns):
+        across = slice(at, at + columns)
+        turned = jnp.transpose(total[:, :, across], (1, 0, 2))
+        for f in range(F):
+            out_ref[f, :, across] = jnp.concatenate([turned[f], turned[F + f]], 0).astype(BF16)
 
 
 def project(nears, pairs, side, x_ref, cos_ref, sin_ref, real_lhs, swap_lhs, power):
@@ -210,10 +213,13 @@
     y, diagonal = project(nears, pairs, 1, x_ref, cos_ref, sin_ref, real_lhs, swap_lhs, power)
     y = y + y_ref[...]
     value = y * y
-    diagonal = diagonal + diagonal_ref[...]
+    if value.shape[1] % LANES:
+        value = jnp.concatenate([value, jnp.zeros((value.shape[0], -value.shape[1] % LANES), F32)], 1)
+    total = -(diagonal + diagonal_ref[...])
+    for lane in range(0, value.shape[1], LANES):
+        total = total + value[:, lane : lane + LANES]
     for block in range(out_ref.shape[1]):
-        rows = slice(block * LANES, (block + 1) * LANES)
-        line = jnp.sum(value[rows].T, axis=0, keepdims=True) - jnp.sum(diagonal[rows].T, axis=0, keepdims=True)
+        line = jnp.sum(total[block * LANES : (block + 1) * LANES].T, axis=0, keepdims=True)
         out_ref[:, block : block + 1, :] = jnp.broadcast_to(line[None], (out_ref.shape[0], 1, LANES))
 
 
@@ -248,7 +254,7 @@
             pltpu.VMEM((half_points, LANES), BF16),
             pltpu.VMEM((DEPTH, total_mics), BF16),
             pltpu.VMEM((snaps, samples, mics), BF16),
-            pltpu.VMEM((2 * F, snaps, mics), F32),
+            pltpu.VMEM((snaps, 2 * F, mics), F32),
             pltpu.SMEM(bins.shape, jnp.int32),
             pltpu.VMEM(mic_positions.shape, F32),
             pltpu.VMEM(grid_positions.shape, F32),

time: 36.1 us -> 35.9 us (level)
  no operation moved by 1% of the time
where the time goes in v6:
time: 35.9 us; the launch traced here: 35.7 us
  blocking collectives  23.2 us (65%)
  Pallas kernels  11.7 us (33%)
  other arithmetic  0.7 us (2%)
    all_to_all x1, blocking collectives, shards(): own = lax.all_to_all(local, ('near', 'pair'), 0, 0, tiled=True)  12.6 us
    all_to_all x1, blocking collectives, shards(): everyone = lax.all_to_all(mine, axes, 0, 0, tiled=True)  10.6 us
    pallas_call x1, Pallas kernels, shards(): pl.pallas_call(functools.partial(dft_kernel, pairs), in_specs=[smem, anyw...  8.65 us
    pallas_call x1, Pallas kernels, shards(): pl.pallas_call(functools.partial(other_kernel, nears, pairs), in_specs=[v...  1.61 us
    pallas_call x1, Pallas kernels, shards(): pl.pallas_call(functools.partial(own_kernel, nears, pairs), in_specs=[vme...  1.47 us
  transfers between devices with their start and end apart: 1, of which 1 were waited for; matrix products, arithmetic and copies ran while one was open for 0% of the time, Pallas kernels for 4%

profile of v6, /device:TPU:0, one launch (start us, length us, event | category | flops | bytes accessed | tf_op | source)
XLA Modules:
  0.0 35.7 jit_solution(16427752900958157591)
XLA Ops:
  0.0 0.1 pad_add_fusion.place_ref
  0.1 8.7 %dft_and_steering.1 = (bf16[8,16,1024]{2,1,0:T(8,128)(2,1)S(1)}, bf16[512,4096]{1,0:T(8,128)(2,1)S(1)}, bf16[512,4096]{1,0:T(8,128)(2,1)S(1)}) custom-call(s32[2]{0:T(128)S(1)} %pad_add_fusion.place_ref, s32[8]{0:T(128)} %bins_hbm.1, f32[3,4096]{1,0:T(4,128)} %mic_hbm.1, f32[3,1024]{1,0:T(4,128)} %grid_hbm.1, bf16[8,1024,1024]{2,1,0:T(8,128)(2,1)} %signal_ref.1), custom_call_target="tpu_custom_call" | custom-call | tf_op jit(solution)/shard_map/dft_and_steering/pallas_call | solution.py:245
  8.7 12.6 %all_to_all.10.x_ref = bf16[8,16,1024]{2,1,0:T(8,128)(2,1)S(1)} all-to-all(bf16[8,16,1024]{2,1,0:T(8,128)(2,1)S(1)} %get-tuple-element.10), channel_id=1, replica_groups=mesh['wide'=2,'near'=4,'pair'=2,'core'=2] {'near','pair'}, dimensions={0} | all-to-all | bytes 524288 | tf_op jit(solution)/shard_map/all_to_all | solution.py:268
  21.3 0.0 collective-permute-start
  21.3 1.5 %own_projection.1 = (f32[512,64]{1,0:T(8,128)S(1)}, f32[512,128]{1,0:T(8,128)S(1)}) custom-call(bf16[8,16,1024]{2,1,0:T(8,128)(2,1)S(1)} %all_to_all.10.x_ref, bf16[512,4096]{1,0:T(8,128)(2,1)S(1)} %get-tuple-element.11.cos_ref, bf16[512,4096]{1,0:T(8,128)(2,1)S(1)} %get-tuple-element.12.sin_ref), custom_call_target="tpu_custom_call" | custom-call | flops 268435456 | bytes 4194304 | tf_op jit(solution)/shard_map/own_projection/pallas_call | solution.py:281
  22.8 0.1 collective-permute-done.x_ref
  22.9 1.6 %other_projection.1 = f32[32,4,128]{2,1,0:T(4,128)S(1)} custom-call(bf16[8,16,1024]{2,1,0:T(8,128)(2,1)S(1)} %collective-permute-done.x_ref, bf16[512,4096]{1,0:T(8,128)(2,1)S(1)} %get-tuple-element.11.cos_ref, bf16[512,4096]{1,0:T(8,128)(2,1)S(1)} %get-tuple-element.12.sin_ref, f32[512,64]{1,0:T(8,128)S(1)} %get-tuple-element.13.y_ref, ...), custom_call_target="tpu_custom_call" | custom-call | flops 268435456 | bytes 4194304 | tf_op jit(solution)/shard_map/other_projection/pallas_call | solution.py:291
  24.5 10.6 %all_to_all.11 = f32[32,4,128]{2,1,0:T(4,128)S(1)} all-to-all(f32[32,4,128]{2,1,0:T(4,128)S(1)} %other_projection.1), channel_id=1, replica_groups=mesh['wide'=2,'near'=4,'pair'=2,'core'=2] {'wide','near','pair','core'}, dimensions={0} | all-to-all | bytes 131072 | tf_op jit(solution)/shard_map/all_to_all | solution.py:302
  35.1 0.6 %broadcast_multiply_fusion = f32[8,1024]{1,0:T(8,128)} fusion(f32[8,1024]{1,0:T(8,128)S(1)} %reduce_sum.9), kind=kLoop, calls=%fused_computation | loop fusion | flops 8192 | bytes 65536 | tf_op jit(solution)/shard_map/mul | solution.py:305
  (2 shorter events, 0.0 us)
Async XLA Ops:
  21.3 1.5 %collective-permute-start = (bf16[8,16,1024]{2,1,0:T(8,128)(2,1)S(1)}, bf16[8,16,1024]{2,1,0:T(8,128)(2,1)S(1)}, u32[]{:S(2)}, u32[]{:S(2)}) collective-permute-start(bf16[8,16,1024]{2,1,0:T(8,128)(2,1)S(1)} %all_to_all.10.x_ref), channel_id=1, source_target_pairs={{0,1},{1,0},{2,3},{3,2},{4,5},{5,4},{6,7},{7,6},{8,9},{9,8},{10,11... | collective-permute-start | bytes 786440 | tf_op jit(solution)/shard_map/ppermute | solution.py:269

commit v7 on v6

--- a/solution.py
+++ b/solution.py
@@ -117,7 +117,7 @@
 
 
 def dft_kernel(
-    pairs, place_ref, bins_hbm, mic_hbm, grid_hbm, signal_ref,
+    pairs, bins_hbm, mic_hbm, grid_hbm, signal_ref,
     out_ref, cos_ref, sin_ref, left_ref, right_ref,
     held, total, bins_ref, mic_ref, grid_ref, rows8, small_sem, sem,
 ):
@@ -136,7 +136,7 @@
         copy(s).start(priority=1)
     for c in small:
         c.wait()
-    index, core = place_ref[0], place_ref[1]
+    index, core = lax.axis_index("near") * pairs + lax.axis_index("pair"), lax.axis_index("core")
     scale = bins_ref[index].astype(F32) * (RATE_OVER_SOUND / samples)
     order = mic_order(pairs, mics, core)
     distance_factors(scale, mic_ref, order, grid_ref, core * (grid_ref.shape[1] // 2), rows8, left_ref, right_ref)
@@ -228,9 +228,7 @@
     total_mics = mic_positions.shape[1]
     points = grid_positions.shape[1]
     half_points = points // 2
-    place = jnp.stack([lax.axis_index("near") * pairs + lax.axis_index("pair"), lax.axis_index("core")]).astype(jnp.int32)
     vmem = pl.BlockSpec(memory_space=pltpu.VMEM)
-    smem = pl.BlockSpec(memory_space=pltpu.SMEM)
     anywhere = pl.BlockSpec(memory_space=pl.ANY)
 
     def steer_shape(count):
@@ -244,7 +242,7 @@
 
     local, cos, sin = pl.pallas_call(
         functools.partial(dft_kernel, pairs),
-        in_specs=[smem, anywhere, anywhere, anywhere, anywhere],
+        in_specs=[anywhere] * 4,
         out_specs=[vmem] * 3,
         out_shape=[
             jax.ShapeDtypeStruct((F, 2 * snaps, mics), BF16),
@@ -264,7 +262,7 @@
         ],
         compiler_params=pltpu.CompilerParams(vmem_limit_bytes=24 * 2**20),
         name="dft_and_steering",
-    )(place, in_hbm(bins), in_hbm(mic_positions), in_hbm(grid_positions), in_hbm(signal))
+    )(in_hbm(bins), in_hbm(mic_positions), in_hbm(grid_positions), in_hbm(signal))
     own = lax.all_to_all(local, ("near", "pair"), 0, 0, tiled=True)
     other = lax.ppermute(own, "core", [(0, 1), (1, 0)])
     wide = nears * 2 * snaps

time: 35.9 us -> 35.2 us (0.981)
  Pallas kernels: 11.7 us -> 11 us
    pallas_call x1, Pallas kernels: 8.65 us -> 8.1 us  [shards(): pl.pallas_call(functools.partial(dft_kernel, pairs), in_specs=[anywhere]...]
where the time goes in v7:
time: 35.2 us; the launch traced here: 35 us
  blocking collectives  23.1 us (66%)
  Pallas kernels  11 us (31%)
  other arithmetic  0.63 us (2%)
    all_to_all x1, blocking collectives, shards(): own = lax.all_to_all(local, ('near', 'pair'), 0, 0, tiled=True)  12.6 us
    all_to_all x1, blocking collectives, shards(): everyone = lax.all_to_all(mine, axes, 0, 0, tiled=True)  10.5 us
    pallas_call x1, Pallas kernels, shards(): pl.pallas_call(functools.partial(dft_kernel, pairs), in_specs=[anywhere]...  8.1 us
    pallas_call x1, Pallas kernels, shards(): pl.pallas_call(functools.partial(other_kernel, nears, pairs), in_specs=[v...  1.52 us
    pallas_call x1, Pallas kernels, shards(): pl.pallas_call(functools.partial(own_kernel, nears, pairs), in_specs=[vme...  1.38 us
  transfers between devices with their start and end apart: 1, of which 1 were waited for; matrix products, arithmetic and copies ran while one was open for 0% of the time, Pallas kernels for 4%

profile of v7, /device:TPU:0, one launch (start us, length us, event | category | flops | bytes accessed | tf_op | source)
XLA Modules:
  0.0 35.0 jit_solution(15678770069500296678)
XLA Ops:
  0.0 8.1 %dft_and_steering.1 = (bf16[8,16,1024]{2,1,0:T(8,128)(2,1)S(1)}, bf16[512,4096]{1,0:T(8,128)(2,1)S(1)}, bf16[512,4096]{1,0:T(8,128)(2,1)S(1)}) custom-call(s32[8]{0:T(128)} %bins_hbm.1, f32[3,4096]{1,0:T(4,128)} %mic_hbm.1, f32[3,1024]{1,0:T(4,128)} %grid_hbm.1, bf16[8,1024,1024]{2,1,0:T(8,128)(2,1)} %signal_ref.1), custom_call_target="tpu_custom_call" | custom-call | tf_op jit(solution)/shard_map/dft_and_steering/pallas_call | solution.py:243
  8.1 12.6 %all_to_all.10.x_ref = bf16[8,16,1024]{2,1,0:T(8,128)(2,1)S(1)} all-to-all(bf16[8,16,1024]{2,1,0:T(8,128)(2,1)S(1)} %get-tuple-element.10), channel_id=1, replica_groups=mesh['wide'=2,'near'=4,'pair'=2,'core'=2] {'near','pair'}, dimensions={0} | all-to-all | bytes 524288 | tf_op jit(solution)/shard_map/all_to_all | solution.py:266
  20.7 0.0 collective-permute-start
  20.7 1.4 %own_projection.1 = (f32[512,64]{1,0:T(8,128)S(1)}, f32[512,128]{1,0:T(8,128)S(1)}) custom-call(bf16[8,16,1024]{2,1,0:T(8,128)(2,1)S(1)} %all_to_all.10.x_ref, bf16[512,4096]{1,0:T(8,128)(2,1)S(1)} %get-tuple-element.11.cos_ref, bf16[512,4096]{1,0:T(8,128)(2,1)S(1)} %get-tuple-element.12.sin_ref), custom_call_target="tpu_custom_call" | custom-call | flops 268435456 | bytes 4194304 | tf_op jit(solution)/shard_map/own_projection/pallas_call | solution.py:279
  22.1 0.1 collective-permute-done.x_ref
  22.2 1.5 %other_projection.1 = f32[32,4,128]{2,1,0:T(4,128)S(1)} custom-call(bf16[8,16,1024]{2,1,0:T(8,128)(2,1)S(1)} %collective-permute-done.x_ref, bf16[512,4096]{1,0:T(8,128)(2,1)S(1)} %get-tuple-element.11.cos_ref, bf16[512,4096]{1,0:T(8,128)(2,1)S(1)} %get-tuple-element.12.sin_ref, f32[512,64]{1,0:T(8,128)S(1)} %get-tuple-element.13.y_ref, ...), custom_call_target="tpu_custom_call" | custom-call | flops 268435456 | bytes 4194304 | tf_op jit(solution)/shard_map/other_projection/pallas_call | solution.py:289
  23.8 10.5 %all_to_all.11 = f32[32,4,128]{2,1,0:T(4,128)S(1)} all-to-all(f32[32,4,128]{2,1,0:T(4,128)S(1)} %other_projection.1), channel_id=1, replica_groups=mesh['wide'=2,'near'=4,'pair'=2,'core'=2] {'wide','near','pair','core'}, dimensions={0} | all-to-all | bytes 131072 | tf_op jit(solution)/shard_map/all_to_all | solution.py:300
  34.4 0.6 %broadcast_multiply_fusion = f32[8,1024]{1,0:T(8,128)} fusion(f32[8,1024]{1,0:T(8,128)S(1)} %reduce_sum.9), kind=kLoop, calls=%fused_computation | loop fusion | flops 8192 | bytes 65536 | tf_op jit(solution)/shard_map/mul | solution.py:303
  (2 shorter events, 0.0 us)
Async XLA Ops:
  20.7 1.5 %collective-permute-start = (bf16[8,16,1024]{2,1,0:T(8,128)(2,1)S(1)}, bf16[8,16,1024]{2,1,0:T(8,128)(2,1)S(1)}, u32[]{:S(2)}, u32[]{:S(2)}) collective-permute-start(bf16[8,16,1024]{2,1,0:T(8,128)(2,1)S(1)} %all_to_all.10.x_ref), channel_id=1, source_target_pairs={{0,1},{1,0},{2,3},{3,2},{4,5},{5,4},{6,7},{7,6},{8,9},{9,8},{10,11... | collective-permute-start | bytes 786440 | tf_op jit(solution)/shard_map/ppermute | solution.py:267

commit v8 on v7

--- a/solution.py
+++ b/solution.py
@@ -130,10 +130,10 @@
     def copy(s):
         return pltpu.make_async_copy(signal_ref.at[s], held.at[s], sem.at[s])
 
+    for s in range(snaps):
+        copy(s).start(priority=1)
     for c in small:
         c.start()
-    for s in range(snaps):
-        copy(s).start(priority=1)
     for c in small:
         c.wait()
     index, core = lax.axis_index("near") * pairs + lax.axis_index("pair"), lax.axis_index("core")
@@ -187,8 +187,8 @@
     form = (((1,), (1,)), ((), ()))
     step = min(COLUMNS, width)
     points = cos_ref.shape[0]
-    y = jnp.zeros((points, real_lhs.shape[0]), F32)
-    diagonal = jnp.zeros((points, LANES), F32)
+    y = 0.0
+    diagonal = 0.0
     for at in range(0, width, step):
         here = slice(at, at + step)
         cos = cos_ref[:, first + at : first + at + step]

time: 35.2 us -> 35.2 us (level)
  no operation moved by 1% of the time
where the time goes in v8:
time: 35.2 us; the launch traced here: 35 us
  blocking collectives  23.1 us (66%)
  Pallas kernels  11 us (31%)
  other arithmetic  0.63 us (2%)
    all_to_all x1, blocking collectives, shards(): own = lax.all_to_all(local, ('near', 'pair'), 0, 0, tiled=True)  12.6 us
    all_to_all x1, blocking collectives, shards(): everyone = lax.all_to_all(mine, axes, 0, 0, tiled=True)  10.5 us
    pallas_call x1, Pallas kernels, shards(): pl.pallas_call(functools.partial(dft_kernel, pairs), in_specs=[anywhere]...  8.1 us
    pallas_call x1, Pallas kernels, shards(): pl.pallas_call(functools.partial(other_kernel, nears, pairs), in_specs=[v...  1.53 us
    pallas_call x1, Pallas kernels, shards(): pl.pallas_call(functools.partial(own_kernel, nears, pairs), in_specs=[vme...  1.38 us
  transfers between devices with their start and end apart: 1, of which 1 were waited for; matrix products, arithmetic and copies ran while one was open for 0% of the time, Pallas kernels for 4%

profile of v8, /device:TPU:0, one launch (start us, length us, event | category | flops | bytes accessed | tf_op | source)
XLA Modules:
  0.0 35.0 jit_solution(7926005190917715349)
XLA Ops:
  0.0 8.1 %dft_and_steering.1 = (bf16[8,16,1024]{2,1,0:T(8,128)(2,1)S(1)}, bf16[512,4096]{1,0:T(8,128)(2,1)S(1)}, bf16[512,4096]{1,0:T(8,128)(2,1)S(1)}) custom-call(s32[8]{0:T(128)} %bins_hbm.1, f32[3,4096]{1,0:T(4,128)} %mic_hbm.1, f32[3,1024]{1,0:T(4,128)} %grid_hbm.1, bf16[8,1024,1024]{2,1,0:T(8,128)(2,1)} %signal_ref.1), custom_call_target="tpu_custom_call" | custom-call | tf_op jit(solution)/shard_map/dft_and_steering/pallas_call | solution.py:243
  8.1 12.6 %all_to_all.10.x_ref = bf16[8,16,1024]{2,1,0:T(8,128)(2,1)S(1)} all-to-all(bf16[8,16,1024]{2,1,0:T(8,128)(2,1)S(1)} %get-tuple-element.10), channel_id=1, replica_groups=mesh['wide'=2,'near'=4,'pair'=2,'core'=2] {'near','pair'}, dimensions={0} | all-to-all | bytes 524288 | tf_op jit(solution)/shard_map/all_to_all | solution.py:266
  20.7 0.0 collective-permute-start
  20.7 1.4 %own_projection.1 = (f32[512,64]{1,0:T(8,128)S(1)}, f32[512,128]{1,0:T(8,128)S(1)}) custom-call(bf16[8,16,1024]{2,1,0:T(8,128)(2,1)S(1)} %all_to_all.10.x_ref, bf16[512,4096]{1,0:T(8,128)(2,1)S(1)} %get-tuple-element.11.cos_ref, bf16[512,4096]{1,0:T(8,128)(2,1)S(1)} %get-tuple-element.12.sin_ref), custom_call_target="tpu_custom_call" | custom-call | flops 268435456 | bytes 4194304 | tf_op jit(solution)/shard_map/own_projection/pallas_call | solution.py:279
  22.1 0.1 collective-permute-done.x_ref
  22.2 1.5 %other_projection.1 = f32[32,4,128]{2,1,0:T(4,128)S(1)} custom-call(bf16[8,16,1024]{2,1,0:T(8,128)(2,1)S(1)} %collective-permute-done.x_ref, bf16[512,4096]{1,0:T(8,128)(2,1)S(1)} %get-tuple-element.11.cos_ref, bf16[512,4096]{1,0:T(8,128)(2,1)S(1)} %get-tuple-element.12.sin_ref, f32[512,64]{1,0:T(8,128)S(1)} %get-tuple-element.13.y_ref, ...), custom_call_target="tpu_custom_call" | custom-call | flops 268435456 | bytes 4194304 | tf_op jit(solution)/shard_map/other_projection/pallas_call | solution.py:289
  23.8 10.5 %all_to_all.11 = f32[32,4,128]{2,1,0:T(4,128)S(1)} all-to-all(f32[32,4,128]{2,1,0:T(4,128)S(1)} %other_projection.1), channel_id=1, replica_groups=mesh['wide'=2,'near'=4,'pair'=2,'core'=2] {'wide','near','pair','core'}, dimensions={0} | all-to-all | bytes 131072 | tf_op jit(solution)/shard_map/all_to_all | solution.py:300
  34.4 0.6 %broadcast_multiply_fusion = f32[8,1024]{1,0:T(8,128)} fusion(f32[8,1024]{1,0:T(8,128)S(1)} %reduce_sum.9), kind=kLoop, calls=%fused_computation | loop fusion | flops 8192 | bytes 65536 | tf_op jit(solution)/shard_map/mul | solution.py:303
  (2 shorter events, 0.0 us)
Async XLA Ops:
  20.7 1.5 %collective-permute-start = (bf16[8,16,1024]{2,1,0:T(8,128)(2,1)S(1)}, bf16[8,16,1024]{2,1,0:T(8,128)(2,1)S(1)}, u32[]{:S(2)}, u32[]{:S(2)}) collective-permute-start(bf16[8,16,1024]{2,1,0:T(8,128)(2,1)S(1)} %all_to_all.10.x_ref), channel_id=1, source_target_pairs={{0,1},{1,0},{2,3},{3,2},{4,5},{5,4},{6,7},{7,6},{8,9},{9,8},{10,11... | collective-permute-start | bytes 786440 | tf_op jit(solution)/shard_map/ppermute | solution.py:267
